TPU v7x, 32 devices: a whole 2x2x4 slice. The times are simulated.
32 devices in a mesh: grp: 2 (over x), blk: 8 (over z, y), ins: 2 (over core).
Axes of the slice: x: 2, y: 2, z: 4, core: 2. Of those that a mesh axis runs over, the one named last changes fastest.
Arguments:
- start_state: float32 [8, 6, 256, 1024], P('ins', None, 'grp', 'blk'), parts along dimension 2, may hold values from -4 to 4
- source_term: float32 [8, 6, 256, 1024], P('ins', None, 'grp', 'blk'), parts along dimension 2, may hold values from -6 to 6
- time_step: float32 [256, 1024], P('grp', 'blk'), parts along dimension 0, may hold values from 0.05 to 0.2
- wall_factor: float32 [256, 1024], P('grp', 'blk'), parts along dimension 0, may hold values from 0.1 to 1
- flux_split: float32 [2, 2, 6, 6], replicated, may hold values from -1.5 to 1.5
- stator_donor: int32 [8, 1024], P('ins', 'blk'), may hold values from 0 to 1023, as said below
- rotor_donor: int32 [8, 1024], P('ins', 'blk'), may hold values from 0 to 1023, as said below
Outputs:
- new_state: float32 [8, 6, 256, 1024], P('ins', None, 'grp', 'blk'), parts along dimension 2
There are 2 independent parts, one for each index of `grp`. A program takes and returns all parts, laid end to end along the dimension named above; an argument that names none is the same for every part. Nothing has to cross between parts.
Inputs may be any that keep to these rules, and one draw needn't show every extreme that they name: For each instance n, stator_donor[n, j] = (j - s_n) mod 1024 for a shift s_n of that instance. For each instance n, rotor_donor[n, j] = (j + s_n) mod 1024 with the same shift s_n as stator_donor.
All inputs are finite; a program needn't handle non-finite values.
Results may differ from a plain program's by a relative error of at most 0.0001.
Values sent between devices are 32-bit elements; how exact they have to be, the bound alone decides.
A program may use at most 128 MiB of HBM per device.

v0:
```python
import jax
import jax.numpy as jnp
from jax import lax
from jax.sharding import PartitionSpec as P

NINST = 8
CI = 128


OMEGA = 1.0
DESTRUCTION = 2.0
SEGMENT_FACTORS = (1.0 / 3.0, 0.5, 1.0)
HIGHEST_PRECISION = lax.Precision.HIGHEST


def padded(cells, sides, width):
    for axis, dim in sides:
        count = lax.axis_size(axis)
        head = lax.slice_in_dim(cells, 0, width, axis=dim)
        tail = lax.slice_in_dim(cells, cells.shape[dim] - width, cells.shape[dim], axis=dim)
        cells = jnp.concatenate(
            [
                lax.ppermute(tail, axis, [(i, (i + 1) % count) for i in range(count)]),
                cells,
                lax.ppermute(head, axis, [((i + 1) % count, i) for i in range(count)]),
            ],
            axis=dim,
        )
    return cells


def spectral_matrix(instances):
    levels = jnp.arange(instances, dtype=jnp.int32)
    offsets = levels[:, None] - levels[None, :]
    angles = jnp.pi * offsets.astype(jnp.float32) / instances
    parity = (1 - 2 * (jnp.abs(offsets) % 2)).astype(jnp.float32)
    denominator = jnp.where(offsets == 0, jnp.float32(1.0), jnp.sin(angles))
    values = 0.5 * OMEGA * parity * jnp.cos(angles) / denominator
    return jnp.where(offsets == 0, jnp.float32(0.0), values)


def apply_matrix(matrix, values):
    return jnp.einsum("vw,nwij->nvij", matrix, values, precision=HIGHEST_PRECISION)


def apply_row(matrix, values):
    return jnp.einsum("vw,nwj->nvj", matrix, values, precision=HIGHEST_PRECISION)


def pick_donors(donor_row, donor_list):
    width = donor_list.shape[1]
    doubled = jnp.concatenate([donor_row, donor_row], axis=2)
    starts = donor_list[:, 0]

    def take_run(row_pair, start_col):
        return lax.dynamic_slice_in_dim(row_pair, start_col, width, 1)

    return jax.vmap(take_run)(doubled, starts)


def time_derivative(current, my_rows):
    return jnp.einsum(
        "nm,mvij->nvij",
        my_rows,
        lax.all_gather(current, "ins", axis=0, tiled=True),
        precision=HIGHEST_PRECISION,
    )


def residual_of(
    current, source_term, wall_factor, flux_split, stator_donor, rotor_donor, my_rows, first_row
):
    row_count = current.shape[2]
    split_rows = CI // 2
    before_row = jnp.zeros_like(current[:, :, 0])
    after_row = jnp.zeros_like(current[:, :, 0])

    def pick_line(place):
        inner = lax.dynamic_index_in_dim(
            current, jnp.clip(place - 1, 0, row_count - 1), 2, keepdims=False
        )
        return jnp.where(
            place == 0, before_row, jnp.where(place == row_count + 1, after_row, inner)
        )

    stator_place = jnp.clip(split_rows - first_row, 0, row_count + 1)
    rotor_place = jnp.clip(split_rows + 1 - first_row, 0, row_count + 1)
    stator_line = pick_line(stator_place)
    rotor_line = pick_line(rotor_place)
    edge_columns = jnp.stack([current[:, :, :, 0], current[:, :, :, -1]], axis=2)
    near_columns = padded(edge_columns, (("blk", 2),), 1)
    boundary = jnp.stack([stator_line, rotor_line])
    gathered = lax.all_gather(boundary, "blk", axis=3, tiled=True)
    plus_axial = apply_matrix(flux_split[0, 0], current)
    minus_axial = apply_matrix(flux_split[0, 1], current)
    plus_before = apply_row(flux_split[0, 0], before_row)
    minus_after = apply_row(flux_split[0, 1], after_row)
    right_axial = plus_axial + jnp.concatenate(
        [minus_axial[:, :, 1:], minus_after[:, :, None]], axis=2
    )
    left_axial = (
        jnp.concatenate([plus_before[:, :, None], plus_axial[:, :, :-1]], axis=2) + minus_axial
    )
    facing_rotor = pick_donors(gathered[1], stator_donor)
    facing_stator = pick_donors(gathered[0], rotor_donor)
    stator_index = jnp.clip(stator_place - 1, 0, row_count - 1)
    rotor_index = jnp.clip(rotor_place - 1, 0, row_count - 1)
    stator_fix = lax.dynamic_index_in_dim(plus_axial, stator_index, 2, keepdims=False) + apply_row(
        flux_split[0, 1], facing_rotor
    )
    rotor_fix = apply_row(flux_split[0, 0], facing_stator) + lax.dynamic_index_in_dim(
        minus_axial, rotor_index, 2, keepdims=False
    )
    global_rows = jnp.arange(row_count, dtype=jnp.int32)
    right_axial = jnp.where(
        (global_rows == split_rows - 1)[None, None, :, None], stator_fix[:, :, None, :], right_axial
    )
    left_axial = jnp.where(
        (global_rows == split_rows)[None, None, :, None], rotor_fix[:, :, None, :], left_axial
    )
    plus_around = apply_matrix(flux_split[1, 0], current)
    minus_around = apply_matrix(flux_split[1, 1], current)
    plus_before_c = apply_row(flux_split[1, 0], near_columns[:, :, 0])
    minus_after_c = apply_row(flux_split[1, 1], near_columns[:, :, -1])
    right_around = plus_around + jnp.concatenate(
        [minus_around[:, :, :, 1:], minus_after_c[:, :, :, None]], axis=3
    )
    left_around = (
        jnp.concatenate([plus_before_c[:, :, :, None], plus_around[:, :, :, :-1]], axis=3)
        + minus_around
    )
    spectral_term = time_derivative(current, my_rows)
    summed = right_axial - left_axial + right_around - left_around + spectral_term - source_term
    turbulent = current[:, 5]
    return summed.at[:, 5].add(DESTRUCTION * turbulent * jnp.abs(turbulent) * wall_factor)


def local(start_state, source_term, time_step, wall_factor, flux_split, stator_donor, rotor_donor):
    local_count = start_state.shape[0]
    spectral = spectral_matrix(NINST)
    first_instance = lax.axis_index("ins") * local_count
    my_rows = lax.dynamic_slice_in_dim(spectral, first_instance, local_count, 0)
    first_row = jnp.int32(0)
    current = start_state
    for factor in SEGMENT_FACTORS:
        current = start_state - factor * time_step * residual_of(
            current,
            source_term,
            wall_factor,
            flux_split,
            stator_donor,
            rotor_donor,
            my_rows,
            first_row,
        )
    return current


def solution(mesh):
    return jax.shard_map(
        local,
        mesh=mesh,
        in_specs=(
            P("ins", None, "grp", "blk"),
            P("ins", None, "grp", "blk"),
            P("grp", "blk"),
            P("grp", "blk"),
            P(),
            P("ins", "blk"),
            P("ins", "blk"),
        ),
        out_specs=P("ins", None, "grp", "blk"),
        check_vma=False,
    )
```

profile of v0, /device:TPU:0, one launch (start us, length us, event | category | flops | bytes accessed | tf_op | source)
XLA Modules:
  0.0 262.0 jit_solution(9346290757383576667)
XLA Ops:
  7.9 1.7 fusion.111
  9.7 2.0 copy.437
  11.7 6.1 %collective-permute-start = (f32[4,6,1,128]{3,1,0,2:T(8,128)S(1)}, f32[4,6,1,128]{3,1,0,2:T(8,128)S(1)}, u32[]{:S(2)}, u32[]{:S(2)}) collective-permute-start(f32[4,6,1,128]{3,1,0,2:T(8,128)S(1)} %bitcast.292), channel_id=1, source_target_pairs={{2,0},{4,2},{6,4},{8,6},{10,8},{12,10},{14,12},{0,14},{3,1},{5,3},... | collective-permute-start | bytes 36872 | tf_op jit(solution)/shard_map/ppermute | solution.py:25
  18.5 26.3 %all_gather.18 = f32[2,4,6,1024]{3,1,2,0:T(4,128)S(1)} all-gather(f32[2,4,6,128]{3,1,2,0:T(4,128)S(1)} %pad_maximum_fusion.12), channel_id=1, replica_groups=mesh['grp'=2,'blk'=8,'ins'=2] {'blk'}, dimensions={3}, use_global_device_ids=true | all-gather | bytes 221184 | tf_op jit(solution)/shard_map/all_gather | solution.py:93
  45.5 3.1 %copy.344 = f32[4,6,2048]{1,0,2:T(4,128)} copy(f32[4,6,2048]{2,0,1:T(4,128)S(1)} %pad_maximum_fusion.7) | data formatting | bytes 393216 | tf_op jit(solution)/shard_map/concatenate | solution.py:52
  48.6 3.5 %copy.336 = f32[4,6,2048]{1,0,2:T(4,128)} copy(f32[4,6,2048]{2,0,1:T(4,128)S(1)} %pad_maximum_fusion.6) | data formatting | bytes 393216 | tf_op jit(solution)/shard_map/concatenate | solution.py:52
  52.1 1.9 gather_fusion.1
  54.0 1.9 gather_fusion
  55.9 2.8 %fusion.26 = f32[4,128,128,6]{2,3,1,0:T(8,128)S(1)} fusion(f32[4,6,128,128]{3,2,1,0:T(8,128)S(1)} %copy-done, f32[1,1,6,6]{3,1,2,0:T(1,128)S(1)} %get-tuple-element.63), kind=kOutput, calls=%fused_computation.38 | convolution fusion | flops 28311552 | bytes 3145872 | tf_op jit(solution)/shard_map/vw,nwij->nvij/dot_general | solution.py:43
  59.0 2.8 %fusion.28 = f32[4,128,128,6]{2,3,1,0:T(8,128)S(1)} fusion(f32[4,6,128,128]{3,2,1,0:T(8,128)S(1)} %copy-done, f32[1,1,6,6]{3,1,2,0:T(1,128)S(1)} %get-tuple-element.64), kind=kOutput, calls=%fused_computation.40 | convolution fusion | flops 28311552 | bytes 3145872 | tf_op jit(solution)/shard_map/vw,nwij->nvij/dot_general | solution.py:43
  62.1 2.8 %fusion.22 = f32[4,128,128,6]{2,3,1,0:T(8,128)S(1)} fusion(f32[4,6,128,128]{3,2,1,0:T(8,128)S(1)} %copy-done, f32[1,1,6,6]{3,1,2,0:T(1,128)S(1)} %get-tuple-element.61), kind=kOutput, calls=%fused_computation.34 | convolution fusion | flops 28311552 | bytes 3145872 | tf_op jit(solution)/shard_map/vw,nwij->nvij/dot_general | solution.py:43
  64.9 3.3 %fusion.24 = f32[4,128,128,6]{2,3,1,0:T(8,128)S(1)} fusion(f32[4,6,128,128]{3,2,1,0:T(8,128)S(1)} %copy-done, f32[1,1,6,6]{3,1,2,0:T(1,128)S(1)} %get-tuple-element.62), kind=kOutput, calls=%fused_computation.36 | convolution fusion | flops 28311552 | bytes 3145872 | tf_op jit(solution)/shard_map/vw,nwij->nvij/dot_general | solution.py:43
  68.2 1.7 copy_bitcast_fusion.10
  69.9 1.7 copy_bitcast_fusion.8
  72.3 1.3 slice.308
  73.6 1.7 slice.312
  75.6 1.7 copy.356
  77.4 1.7 copy.359
  79.1 6.3 %fusion.4 = f32[4,6,128,128]{3,0,2,1:T(4,128)S(1)} fusion(f32[8,6,128,128]{3,2,1,0:T(8,128)} %all-gather.4.cloned.1.call-done, f32[8,8]{1,0:T(8,128)S(1)} %fusion.87, s32[]{:T(128)S(6)} %select_n.106), kind=kOutput, calls=%fused_computation.10 | convolution fusion | flops 37748736 | bytes 4720644 | tf_op jit(solution)/shard_map/nm,mvij->nvij/dot_general | solution.py:62
  85.5 6.0 %fusion.36 = f32[4,6,128,128]{3,2,1,0:T(8,128)S(1)} fusion(f32[4,6,128,128]{3,2,1,0:T(8,128)S(1)} %copy-done.15, f32[4,6,128,128]{3,2,1,0:T(8,128)S(1)} %copy-done.17, f32[4,6,1,128]{3,2,1,0:T(1,128)S(1)} %copy.347, f32[4,6,128,128]{3,2,1,0:T(8,128)} %get-tuple-element.70, f32[4,6,1,128]{3,2,1,0:T(1,128)S(1)} %copy.343, f32[4,6,127,128]{3,2,1,0:T(8,128)} %slice.308, ...), kind=kLoop, calls=%fused_computation.48 | loop fusion | flops 5898240 | bytes 17326336 | tf_op jit(solution)/shard_map/sub | solution.py:133
  91.9 1.1 copy-done.3
  93.1 20.6 %all_gather.20 = f32[2,4,6,1024]{3,0,2,1:T(2,128)S(1)} all-gather(f32[2,4,6,128]{3,0,2,1:T(2,128)S(1)} %pad_maximum_fusion.13), channel_id=1, replica_groups=mesh['grp'=2,'blk'=8,'ins'=2] {'blk'}, dimensions={3}, use_global_device_ids=true | all-gather | bytes 221184 | tf_op jit(solution)/shard_map/all_gather | solution.py:93
  114.0 3.1 %copy.364 = f32[4,6,2048]{1,0,2:T(4,128)} copy(f32[4,6,2048]{2,0,1:T(4,128)S(1)} %pad_maximum_fusion.8) | data formatting | bytes 393216 | tf_op jit(solution)/shard_map/concatenate | solution.py:52
  117.2 2.7 %gather_fusion.2 = f32[4,6,128]{1,0,2:T(4,128)} fusion(f32[4,6,2048]{1,0,2:T(4,128)} %copy.364, s32[4]{0:T(128)S(1)} %fusion.99), kind=kCustom, calls=%fused_computation.2 | custom fusion | bytes 24624 | tf_op jit(solution)/shard_map/vmap()/gather | solution.py:56
  119.9 3.1 %copy.371 = f32[4,6,2048]{1,0,2:T(4,128)} copy(f32[4,6,2048]{2,0,1:T(4,128)S(1)} %pad_maximum_fusion.9) | data formatting | bytes 393216 | tf_op jit(solution)/shard_map/concatenate | solution.py:52
  123.1 2.7 %gather_fusion.3 = f32[4,6,128]{1,0,2:T(4,128)} fusion(f32[4,6,2048]{1,0,2:T(4,128)} %copy.371, s32[4]{0:T(128)} %copy-done.32), kind=kCustom, calls=%fused_computation.3 | custom fusion | bytes 24624 | tf_op jit(solution)/shard_map/vmap()/gather | solution.py:56
  125.8 2.3 fusion.109
  128.1 1.9 copy.378
  130.2 2.8 %fusion.20 = f32[4,128,128,6]{2,3,1,0:T(8,128)S(1)} fusion(f32[4,6,128,128]{3,2,1,0:T(8,128)S(1)} %copy-done.4, f32[1,1,6,6]{3,1,2,0:T(1,128)S(1)} %get-tuple-element.64), kind=kOutput, calls=%fused_computation.32 | convolution fusion | flops 28311552 | bytes 3145872 | tf_op jit(solution)/shard_map/vw,nwij->nvij/dot_general | solution.py:43
  133.4 2.8 %fusion.18 = f32[4,128,128,6]{2,3,1,0:T(8,128)S(1)} fusion(f32[4,6,128,128]{3,2,1,0:T(8,128)S(1)} %copy-done.4, f32[1,1,6,6]{3,1,2,0:T(1,128)S(1)} %get-tuple-element.63), kind=kOutput, calls=%fused_computation.30 | convolution fusion | flops 28311552 | bytes 3145872 | tf_op jit(solution)/shard_map/vw,nwij->nvij/dot_general | solution.py:43
  136.2 2.8 %fusion.14 = f32[4,128,128,6]{2,3,1,0:T(8,128)S(1)} fusion(f32[4,6,128,128]{3,2,1,0:T(8,128)S(1)} %copy-done.4, f32[1,1,6,6]{3,1,2,0:T(1,128)S(1)} %get-tuple-element.61), kind=kOutput, calls=%fused_computation.26 | convolution fusion | flops 28311552 | bytes 3145872 | tf_op jit(solution)/shard_map/vw,nwij->nvij/dot_general | solution.py:43
  139.0 4.1 %fusion.16 = f32[4,128,128,6]{2,3,1,0:T(8,128)} fusion(f32[4,6,128,128]{3,2,1,0:T(8,128)S(1)} %copy-done.4, f32[1,1,6,6]{3,1,2,0:T(1,128)S(1)} %get-tuple-element.62), kind=kOutput, calls=%fused_computation.28 | convolution fusion | flops 28311552 | bytes 3145872 | tf_op jit(solution)/shard_map/vw,nwij->nvij/dot_general | solution.py:43
  144.0 1.4 copy.561
  145.7 1.6 slice.321
  147.3 1.4 slice.317
  148.7 1.9 copy.382
  150.6 2.0 collective-permute-start.3
  152.6 3.0 %copy.559 = f32[4,128,128,6]{2,1,3,0:T(8,128)} copy(f32[4,128,128,6]{2,3,1,0:T(8,128)} %fusion.16) | data formatting | bytes 3145728 | tf_op jit(solution)/shard_map/vw,nwij->nvij/dot_general | solution.py:43
  155.8 1.7 copy.381
  157.6 1.7 copy.385
  159.3 6.3 %fusion.2 = f32[4,6,128,128]{3,0,2,1:T(4,128)S(1)} fusion(f32[8,6,128,128]{3,2,1,0:T(8,128)} %all-gather.6.cloned.1.call-done, f32[8,8]{1,0:T(8,128)S(1)} %copy-done.37, s32[]{:T(128)S(6)} %select_n.106), kind=kOutput, calls=%fused_computation.8 | convolution fusion | flops 37748736 | bytes 4720644 | tf_op jit(solution)/shard_map/nm,mvij->nvij/dot_general | solution.py:62
  165.7 7.2 %fusion.43 = f32[4,6,128,128]{3,2,1,0:T(8,128)S(1)} fusion(f32[4,6,128,128]{3,2,1,0:T(8,128)} %param.14, f32[4,6,1,128]{3,2,1,0:T(1,128)S(1)} %copy-done.30, f32[4,6,1,128]{3,2,1,0:T(1,128)S(1)} %copy-done.27, f32[4,6,127,128]{3,2,1,0:T(8,128)} %slice.317, f32[4,6,127,128]{3,2,1,0:T(8,128)} %bitcast.274, f32[4,6,128,1]{3,2,1,0:T(8,128)} %copy.381, ...), kind=kLoop, calls=%fused_computation.55 | loop fusion | flops 5898240 | bytes 17326336 | tf_op jit(solution)/shard_map/sub | solution.py:133
  174.5 20.0 %all_gather.22 = f32[2,4,6,1024]{3,0,2,1:T(2,128)S(1)} all-gather(f32[2,4,6,128]{3,0,2,1:T(2,128)S(1)} %pad_maximum_fusion.14), channel_id=1, replica_groups=mesh['grp'=2,'blk'=8,'ins'=2] {'blk'}, dimensions={3}, use_global_device_ids=true | all-gather | bytes 221184 | tf_op jit(solution)/shard_map/all_gather | solution.py:93
  194.8 3.1 %copy.390 = f32[4,6,2048]{1,0,2:T(4,128)} copy(f32[4,6,2048]{2,0,1:T(4,128)S(1)} %pad_maximum_fusion.10) | data formatting | bytes 393216 | tf_op jit(solution)/shard_map/concatenate | solution.py:52
  197.9 2.7 %gather_fusion.4 = f32[4,6,128]{1,0,2:T(4,128)} fusion(f32[4,6,2048]{1,0,2:T(4,128)} %copy.390, s32[4]{0:T(128)S(1)} %copy-done.35), kind=kCustom, calls=%fused_computation.4 | custom fusion | bytes 24624 | tf_op jit(solution)/shard_map/vmap()/gather | solution.py:56
  200.7 3.1 %copy.397 = f32[4,6,2048]{1,0,2:T(4,128)} copy(f32[4,6,2048]{2,0,1:T(4,128)S(1)} %pad_maximum_fusion.11) | data formatting | bytes 393216 | tf_op jit(solution)/shard_map/concatenate | solution.py:52
  203.8 2.6 gather_fusion.5
  206.4 2.3 fusion.108
  208.7 1.9 copy.404
  211.1 2.8 %fusion.12 = f32[4,128,128,6]{2,3,1,0:T(8,128)S(1)} fusion(f32[4,6,128,128]{3,2,1,0:T(8,128)S(1)} %copy-done.2, f32[1,1,6,6]{3,1,2,0:T(1,128)S(1)} %get-tuple-element.64), kind=kOutput, calls=%fused_computation.24 | convolution fusion | flops 28311552 | bytes 3145872 | tf_op jit(solution)/shard_map/vw,nwij->nvij/dot_general | solution.py:43
  214.2 2.8 %fusion.10 = f32[4,128,128,6]{2,3,1,0:T(8,128)S(1)} fusion(f32[4,6,128,128]{3,2,1,0:T(8,128)S(1)} %copy-done.2, f32[1,1,6,6]{3,1,2,0:T(1,128)S(1)} %get-tuple-element.63), kind=kOutput, calls=%fused_computation.22 | convolution fusion | flops 28311552 | bytes 3145872 | tf_op jit(solution)/shard_map/vw,nwij->nvij/dot_general | solution.py:43
  217.1 2.8 %fusion.6 = f32[4,128,128,6]{2,3,1,0:T(8,128)S(1)} fusion(f32[4,6,128,128]{3,2,1,0:T(8,128)S(1)} %copy-done.2, f32[1,1,6,6]{3,1,2,0:T(1,128)S(1)} %get-tuple-element.61), kind=kOutput, calls=%fused_computation.18 | convolution fusion | flops 28311552 | bytes 3145872 | tf_op jit(solution)/shard_map/vw,nwij->nvij/dot_general | solution.py:43
  219.9 4.1 %fusion.8 = f32[4,128,128,6]{2,3,1,0:T(8,128)} fusion(f32[4,6,128,128]{3,2,1,0:T(8,128)S(1)} %copy-done.2, f32[1,1,6,6]{3,1,2,0:T(1,128)S(1)} %get-tuple-element.62), kind=kOutput, calls=%fused_computation.20 | convolution fusion | flops 28311552 | bytes 3145872 | tf_op jit(solution)/shard_map/vw,nwij->nvij/dot_general | solution.py:43
  224.8 1.4 copy.557
  226.5 1.6 slice.333
  228.1 1.4 slice.329
  229.5 1.9 copy.408
  231.4 2.0 collective-permute-start.5
  233.4 3.0 %copy.555 = f32[4,128,128,6]{2,1,3,0:T(8,128)} copy(f32[4,128,128,6]{2,3,1,0:T(8,128)} %fusion.8) | data formatting | bytes 3145728 | tf_op jit(solution)/shard_map/vw,nwij->nvij/dot_general | solution.py:43
  236.6 1.7 copy.407
  238.4 1.7 copy.411
  240.2 6.3 %fusion = f32[4,6,128,128]{3,0,2,1:T(4,128)S(1)} fusion(f32[8,6,128,128]{3,2,1,0:T(8,128)} %all-gather.8.cloned.1.call-done, f32[8,8]{1,0:T(8,128)S(1)} %copy-done.38, s32[]{:T(128)S(6)} %select_n.106), kind=kOutput, calls=%fused_computation.6 | convolution fusion | flops 37748736 | bytes 4720644 | tf_op jit(solution)/shard_map/nm,mvij->nvij/dot_general | solution.py:62
  246.6 7.2 %fusion.50 = f32[4,6,128,128]{3,2,1,0:T(8,128)S(1)} fusion(f32[4,6,128,128]{3,2,1,0:T(8,128)} %param.14, f32[4,6,1,128]{3,2,1,0:T(1,128)S(1)} %copy-done.31, f32[4,6,1,128]{3,2,1,0:T(1,128)S(1)} %copy-done.28, f32[4,6,127,128]{3,2,1,0:T(8,128)} %slice.329, f32[4,6,127,128]{3,2,1,0:T(8,128)} %bitcast.273, f32[4,6,128,1]{3,2,1,0:T(8,128)} %copy.407, ...), kind=kLoop, calls=%fused_computation.62 | loop fusion | flops 5898240 | bytes 17326336 | tf_op jit(solution)/shard_map/sub | solution.py:133
  253.9 1.4 multiply_subtract_fusion
  (171 shorter events, 11.3 us)
Async XLA Ops:
  6.5 1.4 copy-start
  6.5 72.5 %all-gather.4.cloned.1.call-start = ((), (), s32[]{:S(2)}) async-start(), calls=%async_computation | async-start | bytes 4718592 | tf_op jit(solution)/shard_map/all_gather | solution.py:65
  7.3 152.0 %all-gather.6.cloned.1.call-start = ((), (), s32[]{:S(2)}) async-start(), calls=%async_computation.1 | async-start | bytes 4718592 | tf_op jit(solution)/shard_map/all_gather | solution.py:65
  9.7 8.8 %copy-start.39 = (f32[2,2,6,6]{3,1,2,0:T(2,128)S(1)}, f32[2,2,6,6]{3,1,2,0:T(2,128)}, u32[]{:S(2)}) copy-start(f32[2,2,6,6]{3,1,2,0:T(2,128)} %param.17) | copy-start | bytes 1732
  11.7 33.1 %copy-start.46 = (s32[4,128]{1,0:T(4,128)S(1)}, s32[4,128]{1,0:T(4,128)}, u32[]{:S(2)}) copy-start(s32[4,128]{1,0:T(4,128)} %param.19) | copy-start | bytes 6148
  11.7 33.3 %copy-start.47 = (s32[4,128]{1,0:T(4,128)S(1)}, s32[4,128]{1,0:T(4,128)}, u32[]{:S(2)}) copy-start(s32[4,128]{1,0:T(4,128)} %param.18) | copy-start | bytes 6148
  11.7 63.7 %collective-permute-start = (f32[4,6,1,128]{3,1,0,2:T(8,128)S(1)}, f32[4,6,1,128]{3,1,0,2:T(8,128)S(1)}, u32[]{:S(2)}, u32[]{:S(2)}) collective-permute-start(f32[4,6,1,128]{3,1,0,2:T(8,128)S(1)} %bitcast.292), channel_id=1, source_target_pairs={{2,0},{4,2},{6,4},{8,6},{10,8},{12,10},{14,12},{0,14},{3,1},{5,3},... | collective-permute-start | bytes 36872 | tf_op jit(solution)/shard_map/ppermute | solution.py:25
  18.4 58.9 %collective-permute-start.1 = (f32[4,6,1,128]{3,1,0,2:T(8,128)S(1)}, f32[4,6,1,128]{3,1,0,2:T(8,128)S(1)}, u32[]{:S(2)}, u32[]{:S(2)}) collective-permute-start(f32[4,6,1,128]{3,1,0,2:T(8,128)S(1)} %bitcast.291), channel_id=1, source_target_pairs={{0,2},{2,4},{4,6},{6,8},{8,10},{10,12},{12,14},{14,0},{1,3},{3,5},... | collective-permute-start | bytes 36872 | tf_op jit(solution)/shard_map/ppermute | solution.py:23
  45.0 7.1 %copy-start.32 = (s32[4]{0:T(128)}, s32[4]{0:T(128)S(1)}, u32[]{:S(2)}) copy-start(s32[4]{0:T(128)S(1)} %fusion.98) | copy-start | bytes 52
  45.1 72.0 %copy-start.34 = (s32[4]{0:T(128)}, s32[4]{0:T(128)S(1)}, u32[]{:S(2)}) copy-start(s32[4]{0:T(128)S(1)} %fusion.99) | copy-start | bytes 52
  45.5 33.6 %copy-start.36 = (f32[8,8]{1,0:T(8,128)}, f32[8,8]{1,0:T(8,128)S(1)}, u32[]{:S(2)}) copy-start(f32[8,8]{1,0:T(8,128)S(1)} %fusion.87) | copy-start | bytes 772
  48.6 7.2 %copy-start.25 = (f32[128,128]{1,0:T(8,128)S(1)}, f32[128,128]{1,0:T(8,128)}, u32[]{:S(2)}) copy-start(f32[128,128]{1,0:T(8,128)} %param.15) | copy-start | bytes 196612
  69.9 2.4 copy-start.16
  71.6 2.0 copy-start.18
  75.4 10.1 %copy-start.26 = (f32[4,6,1,128]{3,2,1,0:T(1,128)}, f32[4,6,1,128]{3,2,1,0:T(1,128)S(1)}, u32[]{:S(2)}) copy-start(f32[4,6,1,128]{3,2,1,0:T(1,128)S(1)} %copy.343) | copy-start | bytes 36868
  75.4 10.1 %copy-start.29 = (f32[4,6,1,128]{3,2,1,0:T(1,128)}, f32[4,6,1,128]{3,2,1,0:T(1,128)S(1)}, u32[]{:S(2)}) copy-start(f32[4,6,1,128]{3,2,1,0:T(1,128)S(1)} %copy.347) | copy-start | bytes 36868
  79.1 6.4 %copy-start.15 = (f32[4,6,128,128]{3,2,1,0:T(8,128)S(1)}, f32[4,6,128,128]{3,2,1,0:T(8,128)}, u32[]{:S(2)}) copy-start(f32[4,6,128,128]{3,2,1,0:T(8,128)} %param.14) | copy-start | bytes 4718596
  79.1 6.4 %copy-start.40 = (pred[128]{0:T(512)(128)(4,1)S(1)}, pred[128]{0:T(512)(128)(4,1)}, u32[]{:S(2)}) copy-start(pred[128]{0:T(512)(128)(4,1)} %get-tuple-element.71) | copy-start | bytes 388
  79.1 6.4 %copy-start.43 = (pred[128]{0:T(512)(128)(4,1)S(1)}, pred[128]{0:T(512)(128)(4,1)}, u32[]{:S(2)}) copy-start(pred[128]{0:T(512)(128)(4,1)} %get-tuple-element.72) | copy-start | bytes 388
  79.1 6.4 %copy-start.17 = (f32[4,6,128,128]{3,2,1,0:T(8,128)S(1)}, f32[4,6,128,128]{3,2,1,0:T(8,128)}, u32[]{:S(2)}) copy-start(f32[4,6,128,128]{3,2,1,0:T(8,128)} %copy-done.16) | copy-start | bytes 4718596
  79.1 6.4 %copy-start.19 = (f32[4,6,128,128]{3,2,1,0:T(8,128)S(1)}, f32[4,6,128,128]{3,2,1,0:T(8,128)}, u32[]{:S(2)}) copy-start(f32[4,6,128,128]{3,2,1,0:T(8,128)} %copy-done.18) | copy-start | bytes 4718596
  85.5 6.0 %copy-start.20 = (f32[128,128]{1,0:T(8,128)S(1)}, f32[128,128]{1,0:T(8,128)}, u32[]{:S(2)}) copy-start(f32[128,128]{1,0:T(8,128)} %param.16) | copy-start | bytes 196612
  91.9 1.1 copy-start.3
  93.1 147.1 %all-gather.8.cloned.1.call-start = ((), (), s32[]{:S(2)}) async-start(), calls=%async_computation.2 | async-start | bytes 4718592 | tf_op jit(solution)/shard_map/all_gather | solution.py:65
  119.9 5.9 %copy-start.4 = (f32[4,6,128,128]{3,2,1,0:T(8,128)S(1)}, f32[4,6,128,128]{3,2,1,0:T(8,128)}, u32[]{:S(2)}) copy-start(f32[4,6,128,128]{3,2,1,0:T(8,128)} %copy-done.3) | copy-start | bytes 4718596
  130.0 3.0 %copy-start.22 = (f32[4,6,128]{1,0,2:T(4,128)S(1)}, f32[4,6,128]{1,0,2:T(4,128)}, u32[]{:S(2)}) copy-start(f32[4,6,128]{1,0,2:T(4,128)} %gather_fusion.2) | copy-start | bytes 36868
  130.0 25.6 %collective-permute-start.2 = (f32[4,6,1,128]{3,1,0,2:T(8,128)S(1)}, f32[4,6,1,128]{3,1,0,2:T(8,128)S(1)}, u32[]{:S(2)}, u32[]{:S(2)}) collective-permute-start(f32[4,6,1,128]{3,1,0,2:T(8,128)S(1)} %copy.379), channel_id=1, source_target_pairs={{2,0},{4,2},{6,4},{8,6},{10,8},{12,10},{14,12},{0,14},{3,1},{5,3},... | collective-permute-start | bytes 36872 | tf_op jit(solution)/shard_map/ppermute | solution.py:25
  133.0 10.9 %copy-start.9 = (f32[4,128,128,6]{2,3,1,0:T(8,128)}, f32[4,128,128,6]{2,3,1,0:T(8,128)S(1)}, u32[]{:S(2)}) copy-start(f32[4,128,128,6]{2,3,1,0:T(8,128)S(1)} %fusion.20) | copy-start | bytes 4718596
  136.2 7.3 %copy-start.11 = (f32[4,128,128,6]{2,3,1,0:T(8,128)}, f32[4,128,128,6]{2,3,1,0:T(8,128)S(1)}, u32[]{:S(2)}) copy-start(f32[4,128,128,6]{2,3,1,0:T(8,128)S(1)} %fusion.18) | copy-start | bytes 4718596
  139.0 6.4 %copy-start.14 = (f32[4,128,128,6]{2,3,1,0:T(8,128)}, f32[4,128,128,6]{2,3,1,0:T(8,128)S(1)}, u32[]{:S(2)}) copy-start(f32[4,128,128,6]{2,3,1,0:T(8,128)S(1)} %fusion.14) | copy-start | bytes 4718596
  139.0 4.1 %copy-start.24 = (f32[4,6,128]{1,0,2:T(4,128)S(1)}, f32[4,6,128]{1,0,2:T(4,128)}, u32[]{:S(2)}) copy-start(f32[4,6,128]{1,0,2:T(4,128)} %gather_fusion.3) | copy-start | bytes 36868
  150.6 6.9 %collective-permute-start.3 = (f32[4,6,1,128]{3,1,0,2:T(8,128)S(1)}, f32[4,6,1,128]{3,1,0,2:T(8,128)S(1)}, u32[]{:S(2)}, u32[]{:S(2)}) collective-permute-start(f32[4,6,1,128]{3,1,0,2:T(8,128)S(1)} %copy.383), channel_id=1, source_target_pairs={{0,2},{2,4},{4,6},{6,8},{8,10},{10,12},{12,14},{14,0},{1,3},{3,5},... | collective-permute-start | bytes 36872 | tf_op jit(solution)/shard_map/ppermute | solution.py:23
  155.7 3.6 %copy-start.37 = (f32[8,8]{1,0:T(8,128)S(1)}, f32[8,8]{1,0:T(8,128)}, u32[]{:S(2)}) copy-start(f32[8,8]{1,0:T(8,128)} %copy-done.36) | copy-start | bytes 772
  159.3 6.4 %copy-start.27 = (f32[4,6,1,128]{3,2,1,0:T(1,128)S(1)}, f32[4,6,1,128]{3,2,1,0:T(1,128)}, u32[]{:S(2)}) copy-start(f32[4,6,1,128]{3,2,1,0:T(1,128)} %copy-done.26) | copy-start | bytes 36868
  159.3 6.4 %copy-start.30 = (f32[4,6,1,128]{3,2,1,0:T(1,128)S(1)}, f32[4,6,1,128]{3,2,1,0:T(1,128)}, u32[]{:S(2)}) copy-start(f32[4,6,1,128]{3,2,1,0:T(1,128)} %copy-done.29) | copy-start | bytes 36868
  159.3 6.4 %copy-start.41 = (pred[128]{0:T(512)(128)(4,1)S(1)}, pred[128]{0:T(512)(128)(4,1)}, u32[]{:S(2)}) copy-start(pred[128]{0:T(512)(128)(4,1)} %get-tuple-element.71) | copy-start | bytes 388
  159.3 6.4 %copy-start.44 = (pred[128]{0:T(512)(128)(4,1)S(1)}, pred[128]{0:T(512)(128)(4,1)}, u32[]{:S(2)}) copy-start(pred[128]{0:T(512)(128)(4,1)} %get-tuple-element.72) | copy-start | bytes 388
  159.3 6.4 %copy-start.10 = (f32[4,128,128,6]{2,3,1,0:T(8,128)S(1)}, f32[4,128,128,6]{2,3,1,0:T(8,128)}, u32[]{:S(2)}) copy-start(f32[4,128,128,6]{2,3,1,0:T(8,128)} %copy-done.9) | copy-start | bytes 4718596
  159.3 6.4 %copy-start.12 = (f32[4,128,128,6]{2,3,1,0:T(8,128)S(1)}, f32[4,128,128,6]{2,3,1,0:T(8,128)}, u32[]{:S(2)}) copy-start(f32[4,128,128,6]{2,3,1,0:T(8,128)} %copy-done.11) | copy-start | bytes 4718596
  173.3 1.1 copy-start.1
  194.8 3.2 %copy-start.35 = (s32[4]{0:T(128)S(1)}, s32[4]{0:T(128)}, u32[]{:S(2)}) copy-start(s32[4]{0:T(128)} %copy-done.34) | copy-start | bytes 52
  200.7 3.2 %copy-start.33 = (s32[4]{0:T(128)S(1)}, s32[4]{0:T(128)}, u32[]{:S(2)}) copy-start(s32[4]{0:T(128)} %copy-done.32) | copy-start | bytes 52
  200.7 5.8 %copy-start.2 = (f32[4,6,128,128]{3,2,1,0:T(8,128)S(1)}, f32[4,6,128,128]{3,2,1,0:T(8,128)}, u32[]{:S(2)}) copy-start(f32[4,6,128,128]{3,2,1,0:T(8,128)} %copy-done.1) | copy-start | bytes 4718596
  210.6 3.3 %copy-start.21 = (f32[4,6,128]{1,0,2:T(4,128)S(1)}, f32[4,6,128]{1,0,2:T(4,128)}, u32[]{:S(2)}) copy-start(f32[4,6,128]{1,0,2:T(4,128)} %gather_fusion.4) | copy-start | bytes 36868
  210.6 25.8 %collective-permute-start.4 = (f32[4,6,1,128]{3,1,0,2:T(8,128)S(1)}, f32[4,6,1,128]{3,1,0,2:T(8,128)S(1)}, u32[]{:S(2)}, u32[]{:S(2)}) collective-permute-start(f32[4,6,1,128]{3,1,0,2:T(8,128)S(1)} %copy.405), channel_id=1, source_target_pairs={{2,0},{4,2},{6,4},{8,6},{10,8},{12,10},{14,12},{0,14},{3,1},{5,3},... | collective-permute-start | bytes 36872 | tf_op jit(solution)/shard_map/ppermute | solution.py:25
  213.9 10.9 %copy-start.5 = (f32[4,128,128,6]{2,3,1,0:T(8,128)}, f32[4,128,128,6]{2,3,1,0:T(8,128)S(1)}, u32[]{:S(2)}) copy-start(f32[4,128,128,6]{2,3,1,0:T(8,128)S(1)} %fusion.12) | copy-start | bytes 4718596
  217.1 7.3 %copy-start.7 = (f32[4,128,128,6]{2,3,1,0:T(8,128)}, f32[4,128,128,6]{2,3,1,0:T(8,128)S(1)}, u32[]{:S(2)}) copy-start(f32[4,128,128,6]{2,3,1,0:T(8,128)S(1)} %fusion.10) | copy-start | bytes 4718596
  219.9 6.4 %copy-start.13 = (f32[4,128,128,6]{2,3,1,0:T(8,128)}, f32[4,128,128,6]{2,3,1,0:T(8,128)S(1)}, u32[]{:S(2)}) copy-start(f32[4,128,128,6]{2,3,1,0:T(8,128)S(1)} %fusion.6) | copy-start | bytes 4718596
  219.9 4.1 %copy-start.23 = (f32[4,6,128]{1,0,2:T(4,128)S(1)}, f32[4,6,128]{1,0,2:T(4,128)}, u32[]{:S(2)}) copy-start(f32[4,6,128]{1,0,2:T(4,128)} %gather_fusion.5) | copy-start | bytes 36868
  231.4 6.9 %collective-permute-start.5 = (f32[4,6,1,128]{3,1,0,2:T(8,128)S(1)}, f32[4,6,1,128]{3,1,0,2:T(8,128)S(1)}, u32[]{:S(2)}, u32[]{:S(2)}) collective-permute-start(f32[4,6,1,128]{3,1,0,2:T(8,128)S(1)} %copy.409), channel_id=1, source_target_pairs={{0,2},{2,4},{4,6},{6,8},{8,10},{10,12},{12,14},{14,0},{1,3},{3,5},... | collective-permute-start | bytes 36872 | tf_op jit(solution)/shard_map/ppermute | solution.py:23
  236.6 3.6 %copy-start.38 = (f32[8,8]{1,0:T(8,128)S(1)}, f32[8,8]{1,0:T(8,128)}, u32[]{:S(2)}) copy-start(f32[8,8]{1,0:T(8,128)} %copy-done.36) | copy-start | bytes 772
  240.1 6.4 %copy-start.28 = (f32[4,6,1,128]{3,2,1,0:T(1,128)S(1)}, f32[4,6,1,128]{3,2,1,0:T(1,128)}, u32[]{:S(2)}) copy-start(f32[4,6,1,128]{3,2,1,0:T(1,128)} %copy-done.26) | copy-start | bytes 36868
  240.1 6.4 %copy-start.31 = (f32[4,6,1,128]{3,2,1,0:T(1,128)S(1)}, f32[4,6,1,128]{3,2,1,0:T(1,128)}, u32[]{:S(2)}) copy-start(f32[4,6,1,128]{3,2,1,0:T(1,128)} %copy-done.29) | copy-start | bytes 36868
  240.1 6.4 %copy-start.42 = (pred[128]{0:T(512)(128)(4,1)S(1)}, pred[128]{0:T(512)(128)(4,1)}, u32[]{:S(2)}) copy-start(pred[128]{0:T(512)(128)(4,1)} %get-tuple-element.71) | copy-start | bytes 388
  240.1 6.4 %copy-start.45 = (pred[128]{0:T(512)(128)(4,1)S(1)}, pred[128]{0:T(512)(128)(4,1)}, u32[]{:S(2)}) copy-start(pred[128]{0:T(512)(128)(4,1)} %get-tuple-element.72) | copy-start | bytes 388
  240.1 6.4 %copy-start.6 = (f32[4,128,128,6]{2,3,1,0:T(8,128)S(1)}, f32[4,128,128,6]{2,3,1,0:T(8,128)}, u32[]{:S(2)}) copy-start(f32[4,128,128,6]{2,3,1,0:T(8,128)} %copy-done.5) | copy-start | bytes 4718596
  240.2 6.4 %copy-start.8 = (f32[4,128,128,6]{2,3,1,0:T(8,128)S(1)}, f32[4,128,128,6]{2,3,1,0:T(8,128)}, u32[]{:S(2)}) copy-start(f32[4,128,128,6]{2,3,1,0:T(8,128)} %copy-done.7) | copy-start | bytes 4718596
Sparse Core Ops, SparseCore 0:
  8.9 14.8 all-gather.3
  93.2 11.9 all-gather.5
  174.6 11.4 all-gather.7
where the time goes:
time: 265 us; the launch traced here: 262 us
  local copies, waits for them, and re-layouts  86.8 us (33%)
  blocking collectives  66.9 us (25%)
  matrix products  58.5 us (22%)
  other arithmetic  23.8 us (9%)
  between operations  14.2 us (5%)
  starting transfers between devices  10.9 us (4%)
    all_gather x3, blocking collectives, residual_of(): gathered = lax.all_gather(boundary, 'blk', axis=3, tiled=True)  66.9 us
    dot_general x12, matrix products, apply_matrix(): jnp.einsum('vw,nwij->nvij', matrix, values, precision=HIGHEST_PRECISION)  36.5 us
    sub x3, other arithmetic, residual_of(): right_axial - left_axial + right_around - left_around + spectral_term  20.5 us
    concatenate x6, local copies, waits for them, and re-layouts, pick_donors(): doubled = jnp.concatenate([donor_row, donor_row], axis=2)  19.2 us
    dot_general x3, matrix products, time_derivative(): jnp.einsum('nm,mvij->nvij', my_rows, lax.all_gather(current, 'ins', axis=...  18.9 us
    gather x6, local copies, waits for them, and re-layouts, take_run(): return lax.dynamic_slice_in_dim(row_pair, start_col, width, 1)  14.4 us
    dot_general x8, local copies, waits for them, and re-layouts, apply_matrix(): jnp.einsum('vw,nwij->nvij', matrix, values, precision=HIGHEST_PRECISION)  10.4 us
    slice x5, local copies, waits for them, and re-layouts, residual_of(): current[:, :, :, -1]  10.1 us
  transfers between devices with their start and end apart: 9, of which 0 were waited for; matrix products, arithmetic and copies ran while one was open for 47% of the time, Pallas kernels for 0%

commit v1 on v0

v1 whole, which is shorter than its diff:
```python
import functools
import math

import jax
import jax.numpy as jnp
from jax import lax
from jax.experimental import pallas as pl
from jax.experimental.pallas import tpu as pltpu
from jax.sharding import PartitionSpec as P

NINST = 8
NV = 6
CHANNELS = NINST * NV
LANES = 128
PITCH_PAD = 8
SEGMENT_FACTORS = (1.0 / 3.0, 0.5, 1.0)
MESH = pl.DeviceIdType.MESH
F32 = jnp.float32
BF16 = jnp.bfloat16


def split_stack(values):
    high = values.astype(BF16)
    low = (values - high.astype(F32)).astype(BF16)
    return jnp.concatenate([high, low, high], axis=0)


def build_weights(flux_ref, weight_ref):
    shape = (NINST, 3 * CHANNELS)
    lane = lax.broadcasted_iota(jnp.int32, shape, 1)
    instance = lax.broadcasted_iota(jnp.int32, shape, 0)
    column = (
        lane
        - jnp.where(lane >= CHANNELS, CHANNELS, 0)
        - jnp.where(lane >= 2 * CHANNELS, CHANNELS, 0)
    )
    in_component = column >> 3
    offset = instance - (column & 7)
    spectral = jnp.zeros(shape, F32)
    for d in range(1, NINST):
        value = 0.5 * (-1.0) ** d * math.cos(math.pi * d / NINST) / math.sin(math.pi * d / NINST)
        spectral = jnp.where(offset == d, F32(value), spectral)
        spectral = jnp.where(offset == -d, F32(-value), spectral)
    same = offset == 0

    def flux_row(direction, part, v):
        row = jnp.zeros(shape, F32)
        for w in range(NV):
            row = jnp.where(in_component == w, flux_ref[direction, part, v, w], row)
        return row

    rows = [[], [], [], [], []]
    for v in range(NV):
        pa, ma = flux_row(0, 0, v), flux_row(0, 1, v)
        pc, mc = flux_row(1, 0, v), flux_row(1, 1, v)
        centre = jnp.where(same, pa - ma + pc - mc, 0.0) + jnp.where(
            in_component == v, spectral, 0.0
        )
        rows[0].append(centre)
        for place, matrix in ((1, ma), (2, -pa), (3, mc), (4, -pc)):
            rows[place].append(jnp.where(same, matrix, 0.0))
    flat = [row for group in rows for row in group]
    for k in range(0, len(flat), 2):
        value = jnp.concatenate([flat[k], flat[k + 1]], axis=0)
        high = value.astype(BF16).astype(F32)
        wide = lax.broadcasted_iota(jnp.int32, value.shape, 1)
        weight_ref[k * 8 : k * 8 + 16, :] = jnp.where(
            wide < 2 * CHANNELS, high, value - high
        ).astype(BF16)


def kernel(
    blocks,
    half,
    start_hbm,
    source_hbm,
    dt_ref,
    wall_ref,
    flux_ref,
    stator_ref,
    rotor_ref,
    out_hbm,
    state0,
    state1,
    state2,
    source,
    weight_ref,
    donors,
    donor_send,
    row_send,
    row_recv,
    edge_send,
    edge_recv,
    local_sem,
    remote_send_sem,
    remote_recv_sem,
    donor_sem,
    row_send_sem,
    row_recv_sem,
    edge_send_sem,
    edge_recv_sem,
):
    me = lax.axis_index("ins")
    blk = lax.axis_index("blk")
    other = 1 - me
    per_core = start_hbm.shape[0]
    pitch = half + PITCH_PAD
    right = lax.rem(blk + 1, blocks)
    left = lax.rem(blk + blocks - 1, blocks)
    my_rows = pl.ds(pl.multiple_of(me * half, 8), half)
    other_rows = pl.ds(pl.multiple_of(other * half, 8), half)

    def local_in(array, place, buffer, n):
        return pltpu.make_async_copy(
            array.at[n, :, my_rows, :],
            buffer.at[:, per_core * me + n, pl.ds(0, half), :],
            local_sem.at[place, n],
        )

    def remote_in(array, place, buffer, n):
        return pltpu.make_async_remote_copy(
            src_ref=array.at[n, :, other_rows, :],
            dst_ref=buffer.at[:, per_core * me + n, pl.ds(0, half), :],
            send_sem=remote_send_sem.at[place, n],
            recv_sem=remote_recv_sem.at[place, n],
            device_id={"ins": other},
            device_id_type=MESH,
        )

    for n in range(per_core):
        local_in(start_hbm, 0, state0, n).start()

    barrier = pltpu.get_barrier_semaphore()
    for b in range(blocks):
        pl.semaphore_signal(barrier, inc=1, device_id={"blk": b, "ins": other}, device_id_type=MESH)
    for b in (left, right):
        pl.semaphore_signal(barrier, inc=1, device_id={"blk": b}, device_id_type=MESH)
    for n in range(per_core):
        local_in(source_hbm, 1, source, n).start()
    build_weights(flux_ref, weight_ref)
    stator = stator_ref[...]
    rotor = rotor_ref[...]
    donors[me] = jnp.where(me == 0, stator, rotor)
    donor_send[...] = jnp.where(me == 0, rotor, stator)
    pl.semaphore_wait(barrier, blocks + 2)

    for n in range(per_core):
        remote_in(start_hbm, 0, state0, n).start()
    donor_copy = pltpu.make_async_remote_copy(
        src_ref=donor_send,
        dst_ref=donors.at[me],
        send_sem=donor_sem.at[0],
        recv_sem=donor_sem.at[1],
        device_id={"ins": other},
        device_id_type=MESH,
    )
    donor_copy.start()
    for n in range(per_core):
        remote_in(source_hbm, 1, source, n).start()

    def row_copy(stage, b):
        return pltpu.make_async_remote_copy(
            src_ref=row_send.at[stage],
            dst_ref=row_recv.at[stage, blk],
            send_sem=row_send_sem.at[stage, b],
            recv_sem=row_recv_sem.at[stage, blk],
            device_id={"blk": b, "ins": other},
            device_id_type=MESH,
        )

    def row_arrival(stage, b):
        return pltpu.make_async_remote_copy(
            src_ref=row_send.at[stage],
            dst_ref=row_recv.at[stage, b],
            send_sem=row_send_sem.at[stage, b],
            recv_sem=row_recv_sem.at[stage, b],
            device_id={"blk": b, "ins": other},
            device_id_type=MESH,
        )

    def edge_copy(stage, side):
        return pltpu.make_async_remote_copy(
            src_ref=edge_send.at[stage],
            dst_ref=edge_recv.at[stage, side],
            send_sem=edge_send_sem.at[stage, side],
            recv_sem=edge_recv_sem.at[stage, side],
            device_id={"blk": right if side == 0 else left},
            device_id_type=MESH,
        )

    def send_row(stage):
        for b in range(blocks):
            row_copy(stage, b).start()

    def send_edges(stage):
        for side in range(2):
            edge_copy(stage, side).start()

    flat = {
        id(buffer): buffer.reshape(CHANNELS * pitch, LANES)
        for buffer in (state0, state1, state2, source)
    }

    def load_row(buffer, i):
        return flat[id(buffer)][pl.ds(i, CHANNELS, stride=pitch), :]

    def store_row(buffer, i, value):
        flat[id(buffer)][pl.ds(i, CHANNELS, stride=pitch), :] = value

    lane = lax.broadcasted_iota(jnp.int32, (CHANNELS, LANES), 1)
    first_lane = lane == 0
    last_lane = lane == LANES - 1
    edge_lane = first_lane | last_lane
    pair_index = lane >> 1
    even_lane = (lane & 1) == 0

    def step_row(i):
        return jnp.broadcast_to(dt_ref[pl.ds(me * half + i, 1), :], (CHANNELS, LANES))

    def wall_row(i):
        return jnp.broadcast_to(wall_ref[pl.ds(me * half + i, 1), :], (NINST, LANES))

    def main_pass(current, target, factor):
        def finish(i, total):
            store_row(
                target, i, load_row(state0, i) - (factor * step_row(i)) * total
            )

        def group(t, carry):
            pending, behind = carry
            first = t * 8
            for pair in range(4):
                rows = (first + 2 * pair, first + 2 * pair + 1)
                cells = [load_row(current, i) for i in rows]
                product = jnp.dot(
                    weight_ref[...],
                    split_stack(jnp.concatenate(cells, axis=1)),
                    preferred_element_type=F32,
                )
                for k in range(2):
                    i = rows[k]
                    centre, ahead, back, mc, pc = [
                        product[
                            CHANNELS * g : CHANNELS * (g + 1), LANES * k : LANES * (k + 1)
                        ]
                        for g in range(5)
                    ]
                    before = i - 1
                    if pair == 0 and k == 0:
                        before = jnp.maximum(before, 0)
                    finish(before, pending + ahead)
                    total = centre + behind - load_row(source, i)
                    total += jnp.where(last_lane, 0.0, pltpu.roll(mc, LANES - 1, axis=1))
                    total += jnp.where(first_lane, 0.0, pltpu.roll(pc, 1, axis=1))
                    turbulent = cells[k][CHANNELS - NINST :, :]
                    extra = 2.0 * turbulent * jnp.abs(turbulent) * wall_row(i)
                    pending = jnp.concatenate(
                        [total[: CHANNELS - NINST], total[CHANNELS - NINST :] + extra], axis=0
                    )
                    behind = back
            return pending, behind

        zero = jnp.zeros((CHANNELS, LANES), F32)
        pending, _ = lax.fori_loop(0, half // 8, group, (zero, zero))
        finish(half - 1, pending)

    interface_row = jnp.where(me == 0, half - 1, 0)

    def halo_products(stage):
        for side in range(2):
            edge_copy(stage, side).wait_recv()
        from_left = pltpu.roll(edge_recv[stage, 0], 1, axis=1)
        from_right = pltpu.roll(edge_recv[stage, 1], LANES - 1, axis=1)
        product = jnp.dot(
            weight_ref[3 * CHANNELS :, :],
            split_stack(jnp.concatenate([from_right, from_left], axis=1)),
            preferred_element_type=F32,
        )
        return jnp.where(even_lane, product[:CHANNELS, :LANES], product[CHANNELS:, LANES:])

    def halo_at(halo, i):
        return jnp.where(edge_lane, pltpu.roll(halo, LANES - 1 - 2 * i, axis=1), 0.0)

    def facing_product(stage):
        for b in range(blocks):
            row_arrival(stage, b).wait_recv()
        donor = jnp.concatenate([donors[0], donors[1]], axis=0)
        start = jnp.broadcast_to(donor[:, 0:1], (NINST, LANES))
        shift = start & (LANES - 1)
        block = start >> 7
        small_lane = lax.broadcasted_iota(jnp.int32, (NINST, LANES), 1)
        following = jnp.where(block == blocks - 1, 0, block + 1)
        wanted = jnp.where(small_lane >= shift, block, following)
        index = (small_lane + shift) & (LANES - 1)
        pieces = []
        for v in range(NV):
            piece = jnp.zeros((NINST, LANES), F32)
            for b in range(blocks):
                piece = jnp.where(
                    wanted == b, row_recv[stage, b, v * NINST : (v + 1) * NINST, :], piece
                )
            pieces.append(jnp.take_along_axis(piece, index, axis=1))
        facing = jnp.concatenate(pieces, axis=0)
        matrix = weight_ref[pl.ds(pl.multiple_of(CHANNELS * (1 + me), 16), CHANNELS), :]
        return jnp.dot(matrix, split_stack(facing), preferred_element_type=F32)

    def edge_pass(target, factor, halo, collect):
        def group(t, edges):
            for k in range(8):
                i = t * 8 + k
                value = load_row(target, i)
                if halo is not None:
                    value = value - (factor * step_row(i)) * halo_at(halo, i)
                    store_row(target, i, value)
                if collect:
                    edges = jnp.where(
                        pair_index == i, pltpu.roll(value, 2 * i + 1, axis=1), edges
                    )
            return edges

        return lax.fori_loop(0, half // 8, group, jnp.zeros((CHANNELS, LANES), F32))

    for n in range(per_core):
        local_in(start_hbm, 0, state0, n).wait()
    for n in range(per_core):
        remote_in(start_hbm, 0, state0, n).wait_recv()
    row_send[0] = load_row(state0, interface_row)
    send_row(0)
    edge_send[0] = edge_pass(state0, 0.0, None, True)
    send_edges(0)
    donor_copy.wait_recv()
    for n in range(per_core):
        local_in(source_hbm, 1, source, n).wait()
    for n in range(per_core):
        remote_in(source_hbm, 1, source, n).wait_recv()

    buffers = (state0, state1, state2, state1)
    for stage, factor in enumerate(SEGMENT_FACTORS):
        target = buffers[stage + 1]
        main_pass(buffers[stage], target, factor)
        halo = halo_products(stage)
        facing = facing_product(stage)
        scale = factor * step_row(interface_row)
        value = load_row(target, interface_row) - scale * facing
        store_row(target, interface_row, value)
        if stage < 2:
            row_send[stage + 1] = value - scale * halo_at(halo, interface_row)
            send_row(stage + 1)
        edges = edge_pass(target, factor, halo, stage < 2)
        if stage < 2:
            edge_send[stage + 1] = edges
            send_edges(stage + 1)

    final = buffers[3]

    def local_out(n):
        return pltpu.make_async_copy(
            final.at[:, per_core * me + n, pl.ds(0, half), :],
            out_hbm.at[n, :, my_rows, :],
            local_sem.at[2, n],
        )

    def remote_out(n):
        return pltpu.make_async_remote_copy(
            src_ref=final.at[:, per_core * other + n, pl.ds(0, half), :],
            dst_ref=out_hbm.at[n, :, my_rows, :],
            send_sem=remote_send_sem.at[2, n],
            recv_sem=remote_recv_sem.at[2, n],
            device_id={"ins": other},
            device_id_type=MESH,
        )

    for n in range(per_core):
        remote_out(n).start()
    for n in range(per_core):
        local_out(n).start()
    donor_copy.wait_send()
    for n in range(per_core):
        remote_in(start_hbm, 0, state0, n).wait_send()
        remote_in(source_hbm, 1, source, n).wait_send()
    for stage in range(3):
        for b in range(blocks):
            row_copy(stage, b).wait_send()
        for side in range(2):
            edge_copy(stage, side).wait_send()
    for n in range(per_core):
        local_out(n).wait()
        remote_out(n).wait()


def solution(mesh):
    blocks = mesh.shape["blk"]

    def local(start_state, source_term, time_step, wall_factor, flux_split, stator, rotor):
        per_core, _, rows, _ = start_state.shape
        half = rows // 2
        pitch = half + PITCH_PAD
        state = pltpu.VMEM((NV, NINST, pitch, LANES), F32)
        whole = pl.BlockSpec(memory_space=pltpu.VMEM)
        return pl.pallas_call(
            functools.partial(kernel, blocks, half),
            out_shape=jax.ShapeDtypeStruct(start_state.shape, F32),
            in_specs=[
                pl.BlockSpec(memory_space=pl.ANY),
                pl.BlockSpec(memory_space=pl.ANY),
                whole,
                whole,
                pl.BlockSpec(memory_space=pltpu.SMEM),
                whole,
                whole,
            ],
            out_specs=pl.BlockSpec(memory_space=pl.ANY),
            scratch_shapes=[
                state,
                state,
                state,
                state,
                pltpu.VMEM((5 * CHANNELS, 3 * CHANNELS), BF16),
                pltpu.VMEM((2, per_core, LANES), jnp.int32),
                pltpu.VMEM((per_core, LANES), jnp.int32),
                pltpu.VMEM((3, CHANNELS, LANES), F32),
                pltpu.VMEM((3, blocks, CHANNELS, LANES), F32),
                pltpu.VMEM((3, CHANNELS, LANES), F32),
                pltpu.VMEM((3, 2, CHANNELS, LANES), F32),
                pltpu.SemaphoreType.DMA((3, per_core)),
                pltpu.SemaphoreType.DMA((3, per_core)),
                pltpu.SemaphoreType.DMA((3, per_core)),
                pltpu.SemaphoreType.DMA((2,)),
                pltpu.SemaphoreType.DMA((3, blocks)),
                pltpu.SemaphoreType.DMA((3, blocks)),
                pltpu.SemaphoreType.DMA((3, 2)),
                pltpu.SemaphoreType.DMA((3, 2)),
            ],
            compiler_params=pltpu.CompilerParams(
                collective_id=0, has_side_effects=True, vmem_limit_bytes=48 * 1024 * 1024
            ),
        )(start_state, source_term, time_step, wall_factor, flux_split, stator, rotor)

    return jax.shard_map(
        local,
        mesh=mesh,
        in_specs=(
            P("ins", None, "grp", "blk"),
            P("ins", None, "grp", "blk"),
            P("grp", "blk"),
            P("grp", "blk"),
            P(),
            P("ins", "blk"),
            P("ins", "blk"),
        ),
        out_specs=P("ins", None, "grp", "blk"),
        check_vma=False,
    )
```

time: 265 us -> 41.8 us (0.16); the launches traced: 262 us -> 41.4 us
  local copies, waits for them, and re-layouts: 86.8 us -> 7.71 us
  blocking collectives: 66.9 us -> 0 us
  matrix products: 58.5 us -> 0 us
  Pallas kernels: 0 us -> 33.7 us
  other arithmetic: 23.8 us -> 0 us
  between operations: 14.2 us -> 0.02 us
  starting transfers between devices: 10.9 us -> 0 us
    all_gather x3 -> x0, blocking collectives: 66.9 us -> none  [residual_of(): gathered = lax.all_gather(boundary, 'blk', axis=3, tiled=True)]
    dot_general x29 -> x0, matrix products: 58.5 us -> none  [the longest x12 36.5 us: apply_matrix(): jnp.einsum('vw,nwij->nvij', matrix, values, precision=HIGHEST_PRECISION)]
    pallas_call x0 -> x1, Pallas kernels: none -> 33.7 us  [local(): pl.pallas_call(functools.partial(kernel, blocks, half), out_shape=jax.Sha...]
    slice x20 -> x0, local copies, waits for them, and re-layouts: 23.3 us -> none  [the longest x5 10.1 us: residual_of(): current[:, :, :, -1]]
    sub x6 -> x0, other arithmetic: 22.3 us -> none  [the longest x3 20.5 us: residual_of(): right_axial - left_axial + right_around - left_around + spectral_term]
    concatenate x6 -> x0, local copies, waits for them, and re-layouts: 19.2 us -> none  [pick_donors(): doubled = jnp.concatenate([donor_row, donor_row], axis=2)]
    gather x6 -> x0, local copies, waits for them, and re-layouts: 14.4 us -> none  [take_run(): return lax.dynamic_slice_in_dim(row_pair, start_col, width, 1)]
    ppermute x6 -> x0, starting transfers between devices: 10.8 us -> none  [the longest x3 6.74 us: padded(): lax.ppermute(head, axis, [((i + 1) % count, i) for i in range(count)])]
  transfers between devices with their start and end apart: 9 -> 0, of which waited for: 0 -> 0; matrix products, arithmetic and copies ran while one was open for 47% -> 0% of each run, Pallas kernels for 0% -> 0%
where the time goes in v1:
time: 41.8 us; the launch traced here: 41.4 us
  Pallas kernels  33.7 us (81%)
  local copies, waits for them, and re-layouts  7.71 us (18%)
    pallas_call x1, Pallas kernels, local(): pl.pallas_call(functools.partial(kernel, blocks, half), out_shape=jax.Sha...  33.7 us
    unnamed x14, local copies, waits for them, and re-layouts  7.71 us

profile of v1, /device:TPU:0, one launch (start us, length us, event | category | flops | bytes accessed | tf_op | source)
XLA Modules:
  0.0 41.4 jit_solution(569397212548146021)
XLA Ops:
  0.0 0.7 %copy.8.flux_ref = f32[2,2,6,6]{3,2,1,0:T(8,128)S(1)} copy(f32[2,2,6,6]{3,1,2,0:T(2,128)} %param.11) | data formatting | bytes 1152 | tf_op args[4]
  0.7 0.0 copy-start
  0.7 1.4 %copy-done = f32[4,6,128,128]{3,2,1,0:T(8,128)S(1)} copy-done((f32[4,6,128,128]{3,2,1,0:T(8,128)S(1)}, f32[4,6,128,128]{3,2,1,0:T(8,128)}, u32[]{:S(2)}) %copy-start) | copy-done | bytes 1572888
  2.1 0.0 copy-start.1
  2.1 1.4 %copy-done.1 = f32[4,6,128,128]{3,2,1,0:T(8,128)S(1)} copy-done((f32[4,6,128,128]{3,2,1,0:T(8,128)S(1)}, f32[4,6,128,128]{3,2,1,0:T(8,128)}, u32[]{:S(2)}) %copy-start.1) | copy-done | bytes 1572888
  3.5 0.0 copy-start.2
  3.5 0.8 %copy-done.2 = f32[128,128]{1,0:T(8,128)S(1)} copy-done((f32[128,128]{1,0:T(8,128)S(1)}, f32[128,128]{1,0:T(8,128)}, u32[]{:S(2)}) %copy-start.2) | copy-done | bytes 65560
  4.4 0.0 copy-start.3
  4.4 0.8 %copy-done.3 = f32[128,128]{1,0:T(8,128)S(1)} copy-done((f32[128,128]{1,0:T(8,128)S(1)}, f32[128,128]{1,0:T(8,128)}, u32[]{:S(2)}) %copy-start.3) | copy-done | bytes 65560
  5.2 0.0 copy-start.4
  5.2 0.7 %copy-done.4 = s32[4,128]{1,0:T(4,128)S(1)} copy-done((s32[4,128]{1,0:T(4,128)S(1)}, s32[4,128]{1,0:T(4,128)}, u32[]{:S(2)}) %copy-start.4) | copy-done | bytes 2072
  5.9 0.0 copy-start.5
  5.9 0.7 %copy-done.5 = s32[4,128]{1,0:T(4,128)S(1)} copy-done((s32[4,128]{1,0:T(4,128)S(1)}, s32[4,128]{1,0:T(4,128)}, u32[]{:S(2)}) %copy-start.5) | copy-done | bytes 2072
  6.6 33.7 %shard_map.73 = f32[4,6,128,128]{3,2,1,0:T(8,128)S(1)} custom-call(f32[4,6,128,128]{3,2,1,0:T(8,128)S(1)} %copy-done, f32[4,6,128,128]{3,2,1,0:T(8,128)S(1)} %copy-done.1, f32[128,128]{1,0:T(8,128)S(1)} %copy-done.2, f32[128,128]{1,0:T(8,128)S(1)} %copy-done.3, f32[2,2,6,6]{3,2,1,0:T(8,128)S(1)} %copy.8.flux_ref, s32[4,128]{1,0:T(4,128)S(1)} %copy-done.4, ...), custom_call_target="tpu_custom_call" | custom-call | tf_op jit(solution)/shard_map/pallas_call | solution.py:400
  40.3 1.1 %copy.10 = f32[4,6,128,128]{3,2,1,0:T(8,128)} copy(f32[4,6,128,128]{3,2,1,0:T(8,128)S(1)} %shard_map.73) | data formatting | bytes 3145728
Async XLA Ops:
  0.7 1.4 %copy-start = (f32[4,6,128,128]{3,2,1,0:T(8,128)S(1)}, f32[4,6,128,128]{3,2,1,0:T(8,128)}, u32[]{:S(2)}) copy-start(f32[4,6,128,128]{3,2,1,0:T(8,128)} %start_hbm.1) | copy-start | bytes 4718596
  2.1 1.4 %copy-start.1 = (f32[4,6,128,128]{3,2,1,0:T(8,128)S(1)}, f32[4,6,128,128]{3,2,1,0:T(8,128)}, u32[]{:S(2)}) copy-start(f32[4,6,128,128]{3,2,1,0:T(8,128)} %source_hbm.1) | copy-start | bytes 4718596
  3.5 0.8 %copy-start.2 = (f32[128,128]{1,0:T(8,128)S(1)}, f32[128,128]{1,0:T(8,128)}, u32[]{:S(2)}) copy-start(f32[128,128]{1,0:T(8,128)} %dt_ref.1) | copy-start | bytes 196612
  4.4 0.8 %copy-start.3 = (f32[128,128]{1,0:T(8,128)S(1)}, f32[128,128]{1,0:T(8,128)}, u32[]{:S(2)}) copy-start(f32[128,128]{1,0:T(8,128)} %wall_ref.1) | copy-start | bytes 196612
  5.2 0.7 %copy-start.4 = (s32[4,128]{1,0:T(4,128)S(1)}, s32[4,128]{1,0:T(4,128)}, u32[]{:S(2)}) copy-start(s32[4,128]{1,0:T(4,128)} %stator_ref.1) | copy-start | bytes 6148
  5.9 0.7 %copy-start.5 = (s32[4,128]{1,0:T(4,128)S(1)}, s32[4,128]{1,0:T(4,128)}, u32[]{:S(2)}) copy-start(s32[4,128]{1,0:T(4,128)} %rotor_ref.1) | copy-start | bytes 6148

commit v2 on v1

--- a/solution.py
+++ b/solution.py
@@ -46,7 +46,7 @@
     def flux_row(direction, part, v):
         row = jnp.zeros(shape, F32)
         for w in range(NV):
-            row = jnp.where(in_component == w, flux_ref[direction, part, v, w], row)
+            row = jnp.where(in_component == w, flux_ref[direction, v, part, w], row)
         return row
 
     rows = [[], [], [], [], []]
@@ -74,12 +74,17 @@
     half,
     start_hbm,
     source_hbm,
+    dt_hbm,
+    wall_hbm,
+    flux_ref,
+    stator_hbm,
+    rotor_hbm,
+    out_hbm,
     dt_ref,
     wall_ref,
-    flux_ref,
     stator_ref,
     rotor_ref,
-    out_hbm,
+    small_sem,
     state0,
     state1,
     state2,
@@ -130,6 +135,14 @@
     for n in range(per_core):
         local_in(start_hbm, 0, state0, n).start()
 
+    small = [
+        pltpu.make_async_copy(stator_hbm, stator_ref, small_sem.at[0]),
+        pltpu.make_async_copy(rotor_hbm, rotor_ref, small_sem.at[1]),
+        pltpu.make_async_copy(dt_hbm.at[my_rows, :], dt_ref, small_sem.at[2]),
+        pltpu.make_async_copy(wall_hbm.at[my_rows, :], wall_ref, small_sem.at[3]),
+    ]
+    for copy in small:
+        copy.start()
     barrier = pltpu.get_barrier_semaphore()
     for b in range(blocks):
         pl.semaphore_signal(barrier, inc=1, device_id={"blk": b, "ins": other}, device_id_type=MESH)
@@ -138,6 +151,8 @@
     for n in range(per_core):
         local_in(source_hbm, 1, source, n).start()
     build_weights(flux_ref, weight_ref)
+    for copy in small:
+        copy.wait()
     stator = stator_ref[...]
     rotor = rotor_ref[...]
     donors[me] = jnp.where(me == 0, stator, rotor)
@@ -215,10 +230,10 @@
     even_lane = (lane & 1) == 0
 
     def step_row(i):
-        return jnp.broadcast_to(dt_ref[pl.ds(me * half + i, 1), :], (CHANNELS, LANES))
+        return jnp.broadcast_to(dt_ref[pl.ds(i, 1), :], (CHANNELS, LANES))
 
     def wall_row(i):
-        return jnp.broadcast_to(wall_ref[pl.ds(me * half + i, 1), :], (NINST, LANES))
+        return jnp.broadcast_to(wall_ref[pl.ds(i, 1), :], (NINST, LANES))
 
     def main_pass(current, target, factor):
         def finish(i, total):
@@ -396,21 +411,26 @@
         half = rows // 2
         pitch = half + PITCH_PAD
         state = pltpu.VMEM((NV, NINST, pitch, LANES), F32)
-        whole = pl.BlockSpec(memory_space=pltpu.VMEM)
+        hbm = pl.BlockSpec(memory_space=pltpu.HBM)
         return pl.pallas_call(
             functools.partial(kernel, blocks, half),
-            out_shape=jax.ShapeDtypeStruct(start_state.shape, F32),
+            out_shape=pltpu.VMEM(start_state.shape, F32),
             in_specs=[
-                pl.BlockSpec(memory_space=pl.ANY),
-                pl.BlockSpec(memory_space=pl.ANY),
-                whole,
-                whole,
+                hbm,
+                hbm,
+                hbm,
+                hbm,
                 pl.BlockSpec(memory_space=pltpu.SMEM),
-                whole,
-                whole,
+                hbm,
+                hbm,
             ],
             out_specs=pl.BlockSpec(memory_space=pl.ANY),
             scratch_shapes=[
+                pltpu.VMEM((half, LANES), F32),
+                pltpu.VMEM((half, LANES), F32),
+                pltpu.VMEM((per_core, LANES), jnp.int32),
+                pltpu.VMEM((per_core, LANES), jnp.int32),
+                pltpu.SemaphoreType.DMA((4,)),
                 state,
                 state,
                 state,
@@ -432,9 +452,9 @@
                 pltpu.SemaphoreType.DMA((3, 2)),
             ],
             compiler_params=pltpu.CompilerParams(
-                collective_id=0, has_side_effects=True, vmem_limit_bytes=48 * 1024 * 1024
+                collective_id=0, has_side_effects=True, vmem_limit_bytes=56 * 1024 * 1024
             ),
-        )(start_state, source_term, time_step, wall_factor, flux_split, stator, rotor)
+        )(start_state, source_term, time_step, wall_factor, flux_split.transpose(0, 2, 1, 3), stator, rotor)
 
     return jax.shard_map(
         local,

time: 41.8 us -> 35.3 us (0.84)
  local copies, waits for them, and re-layouts: 7.71 us -> 1.15 us
    unnamed x14 -> x1, local copies, waits for them, and re-layouts: 7.71 us -> 1.15 us
where the time goes in v2:
time: 35.3 us; the launch traced here: 35.1 us
  Pallas kernels  33.9 us (96%)
  local copies, waits for them, and re-layouts  1.15 us (3%)
    pallas_call x1, Pallas kernels, local(): pl.pallas_call(functools.partial(kernel, blocks, half), out_shape=pltpu.V...  33.9 us
    unnamed x1, local copies, waits for them, and re-layouts  1.15 us

profile of v2, /device:TPU:0, one launch (start us, length us, event | category | flops | bytes accessed | tf_op | source)
XLA Modules:
  0.0 35.1 jit_solution(14878170388245126772)
XLA Ops:
  0.0 33.9 %shard_map.73 = f32[4,6,128,128]{3,2,1,0:T(8,128)S(1)} custom-call(f32[4,6,128,128]{3,2,1,0:T(8,128)} %start_hbm.1, f32[4,6,128,128]{3,2,1,0:T(8,128)} %source_hbm.1, f32[128,128]{1,0:T(8,128)} %dt_hbm.1, f32[128,128]{1,0:T(8,128)} %wall_hbm.1, f32[2,6,2,6]{3,2,1,0:T(2,128)} %bitcast.1, s32[4,128]{1,0:T(4,128)} %stator_hbm.1, s32[4,128]{1,0:T(4,128)} %rotor_hbm.1), custom_call_target="tpu_custom_call" | custom-call | tf_op jit(solution)/shard_map/pallas_call | solution.py:415
  33.9 1.1 %copy.9 = f32[4,6,128,128]{3,2,1,0:T(8,128)} copy(f32[4,6,128,128]{3,2,1,0:T(8,128)S(1)} %shard_map.73) | data formatting | bytes 3145728

commit v3 on v2

--- a/solution.py
+++ b/solution.py
@@ -13,6 +13,7 @@
 CHANNELS = NINST * NV
 LANES = 128
 PITCH_PAD = 8
+GROUP = 16
 SEGMENT_FACTORS = (1.0 / 3.0, 0.5, 1.0)
 MESH = pl.DeviceIdType.MESH
 F32 = jnp.float32
@@ -85,6 +86,16 @@
     stator_ref,
     rotor_ref,
     small_sem,
+    own,
+    first_edge_send,
+    first_edge_recv,
+    first_edge_send_sem,
+    first_edge_recv_sem,
+    first_send,
+    first_recv,
+    first_sem,
+    first_send_sem,
+    first_recv_sem,
     state0,
     state1,
     state2,
@@ -132,9 +143,10 @@
             device_id_type=MESH,
         )
 
-    for n in range(per_core):
-        local_in(start_hbm, 0, state0, n).start()
-
+    first_copy = pltpu.make_async_copy(
+        start_hbm, own.at[:, :, pl.ds(0, 2 * half), :], first_sem
+    )
+    first_copy.start()
     small = [
         pltpu.make_async_copy(stator_hbm, stator_ref, small_sem.at[0]),
         pltpu.make_async_copy(rotor_hbm, rotor_ref, small_sem.at[1]),
@@ -146,8 +158,12 @@
     barrier = pltpu.get_barrier_semaphore()
     for b in range(blocks):
         pl.semaphore_signal(barrier, inc=1, device_id={"blk": b, "ins": other}, device_id_type=MESH)
-    for b in (left, right):
-        pl.semaphore_signal(barrier, inc=1, device_id={"blk": b}, device_id_type=MESH)
+    for d in range(1, blocks):
+        pl.semaphore_signal(
+            barrier, inc=1, device_id={"blk": lax.rem(blk + d, blocks)}, device_id_type=MESH
+        )
+    for n in range(per_core):
+        local_in(start_hbm, 0, state0, n).start()
     for n in range(per_core):
         local_in(source_hbm, 1, source, n).start()
     build_weights(flux_ref, weight_ref)
@@ -157,10 +173,35 @@
     rotor = rotor_ref[...]
     donors[me] = jnp.where(me == 0, stator, rotor)
     donor_send[...] = jnp.where(me == 0, rotor, stator)
-    pl.semaphore_wait(barrier, blocks + 2)
-
-    for n in range(per_core):
-        remote_in(start_hbm, 0, state0, n).start()
+    first_copy.wait()
+    own_channels = per_core * NV
+    own_pitch = 2 * half + PITCH_PAD
+    flat_own = own.reshape(own_channels * own_pitch, LANES)
+
+    def own_row(i):
+        return flat_own[pl.ds(i, own_channels, stride=own_pitch), :]
+
+    first_send[0] = own_row(half)
+    first_send[1] = own_row(half - 1)
+    first_recv[blk, me] = first_send[me]
+    own_pair = lax.broadcasted_iota(jnp.int32, (own_channels, LANES), 1) >> 1
+
+    def collect_own(t, edges):
+        low, high = edges
+        for k in range(8):
+            i = t * 8 + k
+            low = jnp.where(own_pair == i, pltpu.roll(own_row(i), 2 * i + 1, axis=1), low)
+            high = jnp.where(
+                own_pair == i, pltpu.roll(own_row(half + i), 2 * i + 1, axis=1), high
+            )
+        return low, high
+
+    nothing = jnp.zeros((own_channels, LANES), F32)
+    low_edges, high_edges = lax.fori_loop(0, half // 8, collect_own, (nothing, nothing))
+    first_edge_send[0] = low_edges
+    first_edge_send[1] = high_edges
+    pl.semaphore_wait(barrier, 2 * blocks - 1)
+
     donor_copy = pltpu.make_async_remote_copy(
         src_ref=donor_send,
         dst_ref=donors.at[me],
@@ -170,6 +211,57 @@
         device_id_type=MESH,
     )
     donor_copy.start()
+
+    def first_edge_copy(core, side):
+        return pltpu.make_async_remote_copy(
+            src_ref=first_edge_send.at[core],
+            dst_ref=first_edge_recv.at[side, me],
+            send_sem=first_edge_send_sem.at[core, side],
+            recv_sem=first_edge_recv_sem.at[side, me],
+            device_id={"blk": right if side == 0 else left, "ins": core},
+            device_id_type=MESH,
+        )
+
+    def first_edge_arrival(core, side):
+        return pltpu.make_async_remote_copy(
+            src_ref=first_edge_send.at[core],
+            dst_ref=first_edge_recv.at[side, core],
+            send_sem=first_edge_send_sem.at[core, side],
+            recv_sem=first_edge_recv_sem.at[side, core],
+            device_id={"blk": right if side == 0 else left, "ins": core},
+            device_id_type=MESH,
+        )
+
+    first_edges = [(core, side) for core in range(2) for side in range(2)]
+
+    def first_row_copy(core, b):
+        return pltpu.make_async_remote_copy(
+            src_ref=first_send.at[core],
+            dst_ref=first_recv.at[blk, me],
+            send_sem=first_send_sem.at[core, b],
+            recv_sem=first_recv_sem.at[me, blk],
+            device_id={"blk": b, "ins": core},
+            device_id_type=MESH,
+        )
+
+    def first_row_arrival(core, b):
+        return pltpu.make_async_remote_copy(
+            src_ref=first_send.at[core],
+            dst_ref=first_recv.at[b, core],
+            send_sem=first_send_sem.at[core, b],
+            recv_sem=first_recv_sem.at[core, b],
+            device_id={"blk": b, "ins": core},
+            device_id_type=MESH,
+        )
+
+    first_peers = [(me, lax.rem(blk + d, blocks)) for d in range(1, blocks)]
+    first_peers += [(other, lax.rem(blk + d, blocks)) for d in range(blocks)]
+    for core, b in first_peers:
+        first_row_copy(core, b).start()
+    for core, side in first_edges:
+        first_edge_copy(core, side).start()
+    for n in range(per_core):
+        remote_in(start_hbm, 0, state0, n).start()
     for n in range(per_core):
         remote_in(source_hbm, 1, source, n).start()
 
@@ -235,18 +327,24 @@
     def wall_row(i):
         return jnp.broadcast_to(wall_ref[pl.ds(i, 1), :], (NINST, LANES))
 
-    def main_pass(current, target, factor):
-        def finish(i, total):
-            store_row(
-                target, i, load_row(state0, i) - (factor * step_row(i)) * total
-            )
+    def main_pass(current, target, factor, halo, collect):
+        def finish(i, total, edges):
+            value = load_row(state0, i) - (factor * step_row(i)) * total
+            store_row(target, i, value)
+            if collect:
+                edges = jnp.where(pair_index == i, pltpu.roll(value, 2 * i + 1, axis=1), edges)
+            return edges
+
+        def corrected(i):
+            value = load_row(current, i)
+            return value if halo is None else value - halo_at(halo, i)
 
         def group(t, carry):
-            pending, behind = carry
-            first = t * 8
-            for pair in range(4):
+            pending, behind, edges = carry
+            first = t * GROUP
+            for pair in range(GROUP // 2):
                 rows = (first + 2 * pair, first + 2 * pair + 1)
-                cells = [load_row(current, i) for i in rows]
+                cells = [corrected(i) for i in rows]
                 product = jnp.dot(
                     weight_ref[...],
                     split_stack(jnp.concatenate(cells, axis=1)),
@@ -263,7 +361,7 @@
                     before = i - 1
                     if pair == 0 and k == 0:
                         before = jnp.maximum(before, 0)
-                    finish(before, pending + ahead)
+                    edges = finish(before, pending + ahead, edges)
                     total = centre + behind - load_row(source, i)
                     total += jnp.where(last_lane, 0.0, pltpu.roll(mc, LANES - 1, axis=1))
                     total += jnp.where(first_lane, 0.0, pltpu.roll(pc, 1, axis=1))
@@ -273,19 +371,35 @@
                         [total[: CHANNELS - NINST], total[CHANNELS - NINST :] + extra], axis=0
                     )
                     behind = back
-            return pending, behind
+            return pending, behind, edges
 
         zero = jnp.zeros((CHANNELS, LANES), F32)
-        pending, _ = lax.fori_loop(0, half // 8, group, (zero, zero))
-        finish(half - 1, pending)
+        pending, _, edges = lax.fori_loop(0, half // GROUP, group, (zero, zero, zero))
+        return finish(half - 1, pending, edges)
 
     interface_row = jnp.where(me == 0, half - 1, 0)
 
     def halo_products(stage):
-        for side in range(2):
-            edge_copy(stage, side).wait_recv()
-        from_left = pltpu.roll(edge_recv[stage, 0], 1, axis=1)
-        from_right = pltpu.roll(edge_recv[stage, 1], LANES - 1, axis=1)
+        if stage == 0:
+            for core, side in first_edges:
+                first_edge_arrival(core, side).wait_recv()
+            flat_edges = first_edge_recv.reshape(2 * CHANNELS, LANES)
+            arrived = [
+                jnp.concatenate(
+                    [
+                        flat_edges[pl.ds(side * CHANNELS + v, NINST, stride=NV), :]
+                        for v in range(NV)
+                    ],
+                    axis=0,
+                )
+                for side in range(2)
+            ]
+        else:
+            for side in range(2):
+                edge_copy(stage - 1, side).wait_recv()
+            arrived = [edge_recv[stage - 1, side] for side in range(2)]
+        from_left = pltpu.roll(arrived[0], 1, axis=1)
+        from_right = pltpu.roll(arrived[1], LANES - 1, axis=1)
         product = jnp.dot(
             weight_ref[3 * CHANNELS :, :],
             split_stack(jnp.concatenate([from_right, from_left], axis=1)),
@@ -297,8 +411,19 @@
         return jnp.where(edge_lane, pltpu.roll(halo, LANES - 1 - 2 * i, axis=1), 0.0)
 
     def facing_product(stage):
-        for b in range(blocks):
-            row_arrival(stage, b).wait_recv()
+        if stage == 0:
+            for core, b in first_peers:
+                first_row_arrival(core, b).wait_recv()
+        else:
+            for b in range(blocks):
+                row_arrival(stage - 1, b).wait_recv()
+        flat_recv = first_recv.reshape(blocks * CHANNELS, LANES)
+
+        def arrived(b, v):
+            if stage == 0:
+                return flat_recv[pl.ds(b * CHANNELS + v, NINST, stride=NV), :]
+            return row_recv[stage - 1, b, v * NINST : (v + 1) * NINST, :]
+
         donor = jnp.concatenate([donors[0], donors[1]], axis=0)
         start = jnp.broadcast_to(donor[:, 0:1], (NINST, LANES))
         shift = start & (LANES - 1)
@@ -311,38 +436,36 @@
         for v in range(NV):
             piece = jnp.zeros((NINST, LANES), F32)
             for b in range(blocks):
-                piece = jnp.where(
-                    wanted == b, row_recv[stage, b, v * NINST : (v + 1) * NINST, :], piece
-                )
+                piece = jnp.where(wanted == b, arrived(b, v), piece)
             pieces.append(jnp.take_along_axis(piece, index, axis=1))
         facing = jnp.concatenate(pieces, axis=0)
         matrix = weight_ref[pl.ds(pl.multiple_of(CHANNELS * (1 + me), 16), CHANNELS), :]
         return jnp.dot(matrix, split_stack(facing), preferred_element_type=F32)
 
-    def edge_pass(target, factor, halo, collect):
-        def group(t, edges):
+    def compact_steps(t, steps):
+        for k in range(8):
+            i = t * 8 + k
+            row = jnp.broadcast_to(dt_ref[pl.ds(i, 1), :], (NINST, LANES))
+            steps = jnp.where(small_pair == i, pltpu.roll(row, 2 * i + 1, axis=1), steps)
+        return steps
+
+    small_pair = lax.broadcasted_iota(jnp.int32, (NINST, LANES), 1) >> 1
+    edge_steps = lax.fori_loop(0, half // 8, compact_steps, jnp.zeros((NINST, LANES), F32))
+    edge_steps = jnp.concatenate([edge_steps] * NV, axis=0)
+
+    def last_pass(target, halo):
+        def group(t, carry):
             for k in range(8):
                 i = t * 8 + k
-                value = load_row(target, i)
-                if halo is not None:
-                    value = value - (factor * step_row(i)) * halo_at(halo, i)
-                    store_row(target, i, value)
-                if collect:
-                    edges = jnp.where(
-                        pair_index == i, pltpu.roll(value, 2 * i + 1, axis=1), edges
-                    )
-            return edges
-
-        return lax.fori_loop(0, half // 8, group, jnp.zeros((CHANNELS, LANES), F32))
+                store_row(target, i, load_row(target, i) - halo_at(halo, i))
+            return carry
+
+        lax.fori_loop(0, half // 8, group, 0)
 
     for n in range(per_core):
         local_in(start_hbm, 0, state0, n).wait()
     for n in range(per_core):
         remote_in(start_hbm, 0, state0, n).wait_recv()
-    row_send[0] = load_row(state0, interface_row)
-    send_row(0)
-    edge_send[0] = edge_pass(state0, 0.0, None, True)
-    send_edges(0)
     donor_copy.wait_recv()
     for n in range(per_core):
         local_in(source_hbm, 1, source, n).wait()
@@ -350,21 +473,23 @@
         remote_in(source_hbm, 1, source, n).wait_recv()
 
     buffers = (state0, state1, state2, state1)
+    halo = None
     for stage, factor in enumerate(SEGMENT_FACTORS):
         target = buffers[stage + 1]
-        main_pass(buffers[stage], target, factor)
-        halo = halo_products(stage)
-        facing = facing_product(stage)
-        scale = factor * step_row(interface_row)
-        value = load_row(target, interface_row) - scale * facing
+        edges = main_pass(buffers[stage], target, factor, halo, stage < 2)
+        halo = (factor * edge_steps) * halo_products(stage)
+        change = (factor * step_row(interface_row)) * facing_product(stage)
+        value = load_row(target, interface_row) - change
         store_row(target, interface_row, value)
         if stage < 2:
-            row_send[stage + 1] = value - scale * halo_at(halo, interface_row)
-            send_row(stage + 1)
-        edges = edge_pass(target, factor, halo, stage < 2)
-        if stage < 2:
-            edge_send[stage + 1] = edges
-            send_edges(stage + 1)
+            row_send[stage] = value - halo_at(halo, interface_row)
+            send_row(stage)
+            corner = pltpu.roll(change, 2 * interface_row + 1, axis=1)
+            edge_send[stage] = (
+                edges - halo - jnp.where(pair_index == interface_row, corner, 0.0)
+            )
+            send_edges(stage)
+    last_pass(buffers[3], halo)
 
     final = buffers[3]
 
@@ -393,7 +518,11 @@
     for n in range(per_core):
         remote_in(start_hbm, 0, state0, n).wait_send()
         remote_in(source_hbm, 1, source, n).wait_send()
-    for stage in range(3):
+    for core, b in first_peers:
+        first_row_copy(core, b).wait_send()
+    for core, side in first_edges:
+        first_edge_copy(core, side).wait_send()
+    for stage in range(2):
         for b in range(blocks):
             row_copy(stage, b).wait_send()
         for side in range(2):
@@ -431,6 +560,16 @@
                 pltpu.VMEM((per_core, LANES), jnp.int32),
                 pltpu.VMEM((per_core, LANES), jnp.int32),
                 pltpu.SemaphoreType.DMA((4,)),
+                pltpu.VMEM((per_core, NV, rows + PITCH_PAD, LANES), F32),
+                pltpu.VMEM((2, per_core * NV, LANES), F32),
+                pltpu.VMEM((2, 2, per_core * NV, LANES), F32),
+                pltpu.SemaphoreType.DMA((2, 2)),
+                pltpu.SemaphoreType.DMA((2, 2)),
+                pltpu.VMEM((2, per_core * NV, LANES), F32),
+                pltpu.VMEM((blocks, 2, per_core * NV, LANES), F32),
+                pltpu.SemaphoreType.DMA,
+                pltpu.SemaphoreType.DMA((2, blocks)),
+                pltpu.SemaphoreType.DMA((2, blocks)),
                 state,
                 state,
                 state,
@@ -438,18 +577,18 @@
                 pltpu.VMEM((5 * CHANNELS, 3 * CHANNELS), BF16),
                 pltpu.VMEM((2, per_core, LANES), jnp.int32),
                 pltpu.VMEM((per_core, LANES), jnp.int32),
-                pltpu.VMEM((3, CHANNELS, LANES), F32),
-                pltpu.VMEM((3, blocks, CHANNELS, LANES), F32),
-                pltpu.VMEM((3, CHANNELS, LANES), F32),
-                pltpu.VMEM((3, 2, CHANNELS, LANES), F32),
+                pltpu.VMEM((2, CHANNELS, LANES), F32),
+                pltpu.VMEM((2, blocks, CHANNELS, LANES), F32),
+                pltpu.VMEM((2, CHANNELS, LANES), F32),
+                pltpu.VMEM((2, 2, CHANNELS, LANES), F32),
                 pltpu.SemaphoreType.DMA((3, per_core)),
                 pltpu.SemaphoreType.DMA((3, per_core)),
                 pltpu.SemaphoreType.DMA((3, per_core)),
                 pltpu.SemaphoreType.DMA((2,)),
-                pltpu.SemaphoreType.DMA((3, blocks)),
-                pltpu.SemaphoreType.DMA((3, blocks)),
-                pltpu.SemaphoreType.DMA((3, 2)),
-                pltpu.SemaphoreType.DMA((3, 2)),
+                pltpu.SemaphoreType.DMA((2, blocks)),
+                pltpu.SemaphoreType.DMA((2, blocks)),
+                pltpu.SemaphoreType.DMA((2, 2)),
+                pltpu.SemaphoreType.DMA((2, 2)),
             ],
             compiler_params=pltpu.CompilerParams(
                 collective_id=0, has_side_effects=True, vmem_limit_bytes=56 * 1024 * 1024

time: 35.3 us -> 33.9 us (0.960)
  Pallas kernels: 33.9 us -> 32.5 us
    pallas_call x1, Pallas kernels: 33.9 us -> 32.5 us  [local(): pl.pallas_call(functools.partial(kernel, blocks, half), out_shape=pltpu.V...]
where the time goes in v3:
time: 33.9 us; the launch traced here: 33.6 us
  Pallas kernels  32.5 us (96%)
  local copies, waits for them, and re-layouts  1.15 us (3%)
    pallas_call x1, Pallas kernels, local(): pl.pallas_call(functools.partial(kernel, blocks, half), out_shape=pltpu.V...  32.5 us
    unnamed x1, local copies, waits for them, and re-layouts  1.15 us

profile of v3, /device:TPU:0, one launch (start us, length us, event | category | flops | bytes accessed | tf_op | source)
XLA Modules:
  0.0 33.6 jit_solution(1716165380554409775)
XLA Ops:
  0.0 32.5 %shard_map.73 = f32[4,6,128,128]{3,2,1,0:T(8,128)S(1)} custom-call(f32[4,6,128,128]{3,2,1,0:T(8,128)} %start_hbm.1, f32[4,6,128,128]{3,2,1,0:T(8,128)} %source_hbm.1, f32[128,128]{1,0:T(8,128)} %dt_hbm.1, f32[128,128]{1,0:T(8,128)} %wall_hbm.1, f32[2,6,2,6]{3,2,1,0:T(2,128)} %bitcast.1, s32[4,128]{1,0:T(4,128)} %stator_hbm.1, s32[4,128]{1,0:T(4,128)} %rotor_hbm.1), custom_call_target="tpu_custom_call" | custom-call | tf_op jit(solution)/shard_map/pallas_call | solution.py:544
  32.5 1.1 %copy.9 = f32[4,6,128,128]{3,2,1,0:T(8,128)} copy(f32[4,6,128,128]{3,2,1,0:T(8,128)S(1)} %shard_map.73) | data formatting | bytes 3145728

commit v4 on v3

--- a/solution.py
+++ b/solution.py
@@ -14,6 +14,7 @@
 LANES = 128
 PITCH_PAD = 8
 GROUP = 16
+CHUNKS = 4
 SEGMENT_FACTORS = (1.0 / 3.0, 0.5, 1.0)
 MESH = pl.DeviceIdType.MESH
 F32 = jnp.float32
@@ -86,6 +87,7 @@
     stator_ref,
     rotor_ref,
     small_sem,
+    out_sem,
     own,
     first_edge_send,
     first_edge_recv,
@@ -414,9 +416,6 @@
         if stage == 0:
             for core, b in first_peers:
                 first_row_arrival(core, b).wait_recv()
-        else:
-            for b in range(blocks):
-                row_arrival(stage - 1, b).wait_recv()
         flat_recv = first_recv.reshape(blocks * CHANNELS, LANES)
 
         def arrived(b, v):
@@ -432,12 +431,12 @@
         following = jnp.where(block == blocks - 1, 0, block + 1)
         wanted = jnp.where(small_lane >= shift, block, following)
         index = (small_lane + shift) & (LANES - 1)
-        pieces = []
-        for v in range(NV):
-            piece = jnp.zeros((NINST, LANES), F32)
-            for b in range(blocks):
-                piece = jnp.where(wanted == b, arrived(b, v), piece)
-            pieces.append(jnp.take_along_axis(piece, index, axis=1))
+        pieces = [jnp.zeros((NINST, LANES), F32)] * NV
+        for b in range(blocks):
+            if stage > 0:
+                row_arrival(stage - 1, b).wait_recv()
+            pieces = [jnp.where(wanted == b, arrived(b, v), pieces[v]) for v in range(NV)]
+        pieces = [jnp.take_along_axis(piece, index, axis=1) for piece in pieces]
         facing = jnp.concatenate(pieces, axis=0)
         matrix = weight_ref[pl.ds(pl.multiple_of(CHANNELS * (1 + me), 16), CHANNELS), :]
         return jnp.dot(matrix, split_stack(facing), preferred_element_type=F32)
@@ -453,14 +452,40 @@
     edge_steps = lax.fori_loop(0, half // 8, compact_steps, jnp.zeros((NINST, LANES), F32))
     edge_steps = jnp.concatenate([edge_steps] * NV, axis=0)
 
+    final = state1
+    chunk = half // CHUNKS
+
+    def local_out(c, n):
+        return pltpu.make_async_copy(
+            final.at[:, per_core * me + n, pl.ds(c * chunk, chunk), :],
+            out_hbm.at[n, :, pl.ds(pl.multiple_of(me * half + c * chunk, 8), chunk), :],
+            out_sem.at[0, c, n],
+        )
+
+    def remote_out(c, n):
+        return pltpu.make_async_remote_copy(
+            src_ref=final.at[:, per_core * other + n, pl.ds(c * chunk, chunk), :],
+            dst_ref=out_hbm.at[n, :, pl.ds(pl.multiple_of(me * half + c * chunk, 8), chunk), :],
+            send_sem=out_sem.at[1, c, n],
+            recv_sem=out_sem.at[2, c, n],
+            device_id={"ins": other},
+            device_id_type=MESH,
+        )
+
     def last_pass(target, halo):
-        def group(t, carry):
-            for k in range(8):
-                i = t * 8 + k
-                store_row(target, i, load_row(target, i) - halo_at(halo, i))
-            return carry
-
-        lax.fori_loop(0, half // 8, group, 0)
+        for c in range(CHUNKS):
+
+            def group(t, carry):
+                for k in range(8):
+                    i = c * chunk + t * 8 + k
+                    store_row(target, i, load_row(target, i) - halo_at(halo, i))
+                return carry
+
+            lax.fori_loop(0, chunk // 8, group, 0)
+            for n in range(per_core):
+                remote_out(c, n).start()
+            for n in range(per_core):
+                local_out(c, n).start()
 
     for n in range(per_core):
         local_in(start_hbm, 0, state0, n).wait()
@@ -491,29 +516,6 @@
             send_edges(stage)
     last_pass(buffers[3], halo)
 
-    final = buffers[3]
-
-    def local_out(n):
-        return pltpu.make_async_copy(
-            final.at[:, per_core * me + n, pl.ds(0, half), :],
-            out_hbm.at[n, :, my_rows, :],
-            local_sem.at[2, n],
-        )
-
-    def remote_out(n):
-        return pltpu.make_async_remote_copy(
-            src_ref=final.at[:, per_core * other + n, pl.ds(0, half), :],
-            dst_ref=out_hbm.at[n, :, my_rows, :],
-            send_sem=remote_send_sem.at[2, n],
-            recv_sem=remote_recv_sem.at[2, n],
-            device_id={"ins": other},
-            device_id_type=MESH,
-        )
-
-    for n in range(per_core):
-        remote_out(n).start()
-    for n in range(per_core):
-        local_out(n).start()
     donor_copy.wait_send()
     for n in range(per_core):
         remote_in(start_hbm, 0, state0, n).wait_send()
@@ -527,9 +529,10 @@
             row_copy(stage, b).wait_send()
         for side in range(2):
             edge_copy(stage, side).wait_send()
-    for n in range(per_core):
-        local_out(n).wait()
-        remote_out(n).wait()
+    for c in range(CHUNKS):
+        for n in range(per_core):
+            local_out(c, n).wait()
+            remote_out(c, n).wait()
 
 
 def solution(mesh):
@@ -560,6 +563,7 @@
                 pltpu.VMEM((per_core, LANES), jnp.int32),
                 pltpu.VMEM((per_core, LANES), jnp.int32),
                 pltpu.SemaphoreType.DMA((4,)),
+                pltpu.SemaphoreType.DMA((3, CHUNKS, per_core)),
                 pltpu.VMEM((per_core, NV, rows + PITCH_PAD, LANES), F32),
                 pltpu.VMEM((2, per_core * NV, LANES), F32),
                 pltpu.VMEM((2, 2, per_core * NV, LANES), F32),
@@ -581,9 +585,9 @@
                 pltpu.VMEM((2, blocks, CHANNELS, LANES), F32),
                 pltpu.VMEM((2, CHANNELS, LANES), F32),
                 pltpu.VMEM((2, 2, CHANNELS, LANES), F32),
-                pltpu.SemaphoreType.DMA((3, per_core)),
-                pltpu.SemaphoreType.DMA((3, per_core)),
-                pltpu.SemaphoreType.DMA((3, per_core)),
+                pltpu.SemaphoreType.DMA((2, per_core)),
+                pltpu.SemaphoreType.DMA((2, per_core)),
+                pltpu.SemaphoreType.DMA((2, per_core)),
                 pltpu.SemaphoreType.DMA((2,)),
                 pltpu.SemaphoreType.DMA((2, blocks)),
                 pltpu.SemaphoreType.DMA((2, blocks)),

time: 33.9 us -> 33.4 us (0.985)
  Pallas kernels: 32.5 us -> 32 us
    pallas_call x1, Pallas kernels: 32.5 us -> 32 us  [local(): pl.pallas_call(functools.partial(kernel, blocks, half), out_shape=pltpu.V...]
where the time goes in v4:
time: 33.4 us; the launch traced here: 33.1 us
  Pallas kernels  32 us (96%)
  local copies, waits for them, and re-layouts  1.15 us (3%)
    pallas_call x1, Pallas kernels, local(): pl.pallas_call(functools.partial(kernel, blocks, half), out_shape=pltpu.V...  32 us
    unnamed x1, local copies, waits for them, and re-layouts  1.15 us

profile of v4, /device:TPU:0, one launch (start us, length us, event | category | flops | bytes accessed | tf_op | source)
XLA Modules:
  0.0 33.1 jit_solution(2423110427743967084)
XLA Ops:
  0.0 32.0 %shard_map.73 = f32[4,6,128,128]{3,2,1,0:T(8,128)S(1)} custom-call(f32[4,6,128,128]{3,2,1,0:T(8,128)} %start_hbm.1, f32[4,6,128,128]{3,2,1,0:T(8,128)} %source_hbm.1, f32[128,128]{1,0:T(8,128)} %dt_hbm.1, f32[128,128]{1,0:T(8,128)} %wall_hbm.1, f32[2,6,2,6]{3,2,1,0:T(2,128)} %bitcast.1, s32[4,128]{1,0:T(4,128)} %stator_hbm.1, s32[4,128]{1,0:T(4,128)} %rotor_hbm.1), custom_call_target="tpu_custom_call" | custom-call | tf_op jit(solution)/shard_map/pallas_call | solution.py:547
  32.0 1.1 %copy.9 = f32[4,6,128,128]{3,2,1,0:T(8,128)} copy(f32[4,6,128,128]{3,2,1,0:T(8,128)S(1)} %shard_map.73) | data formatting | bytes 3145728

commit v5 on v4

--- a/solution.py
+++ b/solution.py
@@ -508,12 +508,12 @@
         store_row(target, interface_row, value)
         if stage < 2:
             row_send[stage] = value - halo_at(halo, interface_row)
-            send_row(stage)
             corner = pltpu.roll(change, 2 * interface_row + 1, axis=1)
             edge_send[stage] = (
                 edges - halo - jnp.where(pair_index == interface_row, corner, 0.0)
             )
             send_edges(stage)
+            send_row(stage)
     last_pass(buffers[3], halo)
 
     donor_copy.wait_send()

time: 33.4 us -> 31.2 us (0.934)
  Pallas kernels: 32 us -> 29.8 us
    pallas_call x1, Pallas kernels: 32 us -> 29.8 us  [local(): pl.pallas_call(functools.partial(kernel, blocks, half), out_shape=pltpu.V...]
where the time goes in v5:
time: 31.2 us; the launch traced here: 30.9 us
  Pallas kernels  29.8 us (96%)
  local copies, waits for them, and re-layouts  1.15 us (4%)
    pallas_call x1, Pallas kernels, local(): pl.pallas_call(functools.partial(kernel, blocks, half), out_shape=pltpu.V...  29.8 us
    unnamed x1, local copies, waits for them, and re-layouts  1.15 us

profile of v5, /device:TPU:0, one launch (start us, length us, event | category | flops | bytes accessed | tf_op | source)
XLA Modules:
  0.0 30.9 jit_solution(7135181896696260766)
XLA Ops:
  0.0 29.8 %shard_map.73 = f32[4,6,128,128]{3,2,1,0:T(8,128)S(1)} custom-call(f32[4,6,128,128]{3,2,1,0:T(8,128)} %start_hbm.1, f32[4,6,128,128]{3,2,1,0:T(8,128)} %source_hbm.1, f32[128,128]{1,0:T(8,128)} %dt_hbm.1, f32[128,128]{1,0:T(8,128)} %wall_hbm.1, f32[2,6,2,6]{3,2,1,0:T(2,128)} %bitcast.1, s32[4,128]{1,0:T(4,128)} %stator_hbm.1, s32[4,128]{1,0:T(4,128)} %rotor_hbm.1), custom_call_target="tpu_custom_call" | custom-call | tf_op jit(solution)/shard_map/pallas_call | solution.py:547
  29.8 1.1 %copy.9 = f32[4,6,128,128]{3,2,1,0:T(8,128)} copy(f32[4,6,128,128]{3,2,1,0:T(8,128)S(1)} %shard_map.73) | data formatting | bytes 3145728
